TPU v7x, 512 devices: a whole 4x4x16 slice. The times are simulated.
512 devices in a mesh: ctx: 64 (over z, y), tp: 8 (over x, core).
Axes of the slice: x: 4, y: 4, z: 16, core: 2. Of those that a mesh axis runs over, the one named last changes fastest.
Arguments:
- queries: bfloat16 [16384, 8192], P('ctx', 'tp'), may hold values from -6 to 6
- keys_values: bfloat16 [2, 16384, 1024], P(None, 'ctx', 'tp'), may hold values from -6 to 6
- segments: int32 [16384], P('ctx'), may hold values from 0 to 15, never falling along the last dimension, each value on 1 to 4096 neighbouring positions
Outputs:
- attended: bfloat16 [16384, 8192], P('ctx', 'tp')
Inputs may be any that keep to these rules, and one draw needn't show every extreme that they name: `segments`: document ids never fall along the tokens; every document holds 1 to 4096 tokens, and one holds exactly 4096.
All inputs are finite; a program needn't handle non-finite values.
Results may differ from a plain program's by a relative error of at most 0.012.
Values may be sent and summed in bfloat16 or wider, within the bound.
No kernel may reach another device: no remote copies, remote signals or barrier semaphores. Data moves between devices by JAX's collectives and lax.ppermute only.
A program may use at most 64 MiB of HBM per device.

v0:
```python
import jax
import jax.numpy as jnp
from jax import lax
from jax.sharding import PartitionSpec as P

HD = 128
REACH = 16


def shifted(x, axis, by):
    length = lax.axis_size(axis)
    pairs = [(i, i + by) for i in range(length) if 0 <= i + by < length]
    return lax.ppermute(x, axis, pairs)


def attend_piece(carried, grouped, query_docs, kv_piece, piece_docs, diagonal_block):
    running_max, row_total, summed = carried
    key_count = kv_piece.shape[1]
    kv_dev = grouped.shape[1]
    key_rows = kv_piece[0].reshape(key_count, kv_dev, HD)
    value_rows = kv_piece[1].reshape(key_count, kv_dev, HD)
    scores = jnp.einsum(
        "tkgd,nkd->kgtn", grouped, key_rows, preferred_element_type=jnp.float32
    ) * HD ** (-0.5)
    visible = query_docs[:, None] == piece_docs[None, :]
    if diagonal_block:
        row_count = grouped.shape[0]
        visible = visible & (jnp.arange(key_count)[None, :] <= jnp.arange(row_count)[:, None])
    scores = jnp.where(visible[None, None], scores, -jnp.inf)
    newest = jnp.maximum(running_max, jnp.max(scores, axis=-1))
    factor = jnp.exp(running_max - newest)
    weights = jnp.exp(scores - newest[..., None])
    row_total = row_total * factor + jnp.sum(weights, axis=-1)
    summed = summed * factor[..., None] + jnp.einsum(
        "kgtn,nkd->kgtd",
        weights.astype(jnp.bfloat16),
        value_rows,
        preferred_element_type=jnp.float32,
    )
    return (newest, row_total, summed)


def on_device(queries, keys_values, segments):
    tok_rows = queries.shape[0]
    kv_dev = keys_values.shape[2] // HD
    group_size = queries.shape[1] // HD // kv_dev
    grouped = queries.reshape(tok_rows, kv_dev, group_size, HD)
    own_docs = segments.astype(jnp.bfloat16)
    my_index = lax.axis_index("ctx")
    carried = (
        jnp.full((kv_dev, group_size, tok_rows), -jnp.inf, jnp.float32),
        jnp.zeros((kv_dev, group_size, tok_rows), jnp.float32),
        jnp.zeros((kv_dev, group_size, tok_rows, HD), jnp.float32),
    )
    carried = attend_piece(carried, grouped, segments, keys_values, segments, True)

    def far_piece(carried, kv_piece, piece_docs, distance):
        source = my_index - distance
        needed = (source >= 0) & (piece_docs[tok_rows - 1] == own_docs[0])

        def compute(state):
            return attend_piece(state, grouped, own_docs, kv_piece, piece_docs, False)

        def keep(state):
            return state

        return lax.cond(needed, compute, keep, carried)

    def advance(loop_state, distance):
        state, moving, moving_docs = loop_state
        moving, moving_docs = shifted((moving, moving_docs), "ctx", 1)
        return ((far_piece(state, moving, moving_docs, distance), moving, moving_docs), None)

    (carried, moving, moving_docs), unused = lax.scan(
        advance, (carried, keys_values, own_docs), jnp.arange(1, REACH + 1)
    )
    running_max, row_total, summed = carried
    return (
        (summed / row_total[..., None])
        .transpose(2, 0, 1, 3)
        .reshape(tok_rows, -1)
        .astype(jnp.bfloat16)
    )


def solution(mesh):
    return jax.shard_map(
        on_device,
        mesh=mesh,
        in_specs=(P("ctx", "tp"), P(None, "ctx", "tp"), P("ctx")),
        out_specs=P("ctx", "tp"),
        check_vma=False,
    )
```

profile of v0, /device:TPU:128, one launch (start us, length us, event | category | flops | bytes accessed | tf_op | source)
XLA Modules:
  0.0 228.7 jit_solution(5789543422403269302)
XLA Ops:
  4.9 222.2 %while.18 = (s32[]{:T(128)}, f32[1,8,256]{2,1,0:T(8,128)S(1)}, f32[1,8,256]{2,1,0:T(8,128)S(1)}, f32[1,8,256,128]{3,2,1,0:T(8,128)S(1)}, bf16[2,256,128]{2,1,0:T...) while((s32[]{:T(128)}, f32[1,8,256]{2,1,0:T(8,128)S(1)}, ...), condition=%wide.region_7.8_spmd, body=%wide.region_2.7_spmd.sunk | while | flops 272701440 | bytes 10096999 | solution.py:74
  4.9 3.5 %collective-permute-start.1 = (bf16[2,256,128]{2,1,0:T(8,128)(2,1)S(1)}, bf16[2,256,128]{2,1,0:T(8,128)(2,1)S(1)}, u32[]{:S(2)}, u32[]{:S(2)}) collective-permute-start(bf16[2,256,128]{2,1,0:T(8,128)(2,1)S(1)} %get-tuple-element.215), channel_id=1, source_target_pairs={{0,8},{8,16},{16,24},{24,32},{32,40},{40,48},{48,56},{56,64},{64,7... | collective-permute-start | bytes 393224 | tf_op jit(solution)/shard_map/while/body/eval_jaxpr/ppermute | solution.py:13
  8.4 3.5 %collective-permute-start = (bf16[256]{0:T(256)(128)(2,1)S(1)}, bf16[256]{0:T(256)(128)(2,1)S(1)}, u32[]{:S(2)}, u32[]{:S(2)}) collective-permute-start(bf16[256]{0:T(256)(128)(2,1)S(1)} %get-tuple-element.216), channel_id=1, source_target_pairs={{0,8},{8,16},{16,24},{24,32},{32,40},{40,48},{48,56},{56,64},{64,7... | collective-permute-start | bytes 1544 | tf_op jit(solution)/shard_map/while/body/eval_jaxpr/ppermute | solution.py:13
  13.0 4.1 %collective-permute-done = bf16[256]{0:T(256)(128)(2,1)S(1)} collective-permute-done((bf16[256]{0:T(256)(128)(2,1)S(1)}, bf16[256]{0:T(256)(128)(2,1)S(1)}, u32[]{:S(2)}, u32[]{:S(2)}) %collective-permute-start) | collective-permute-done | bytes 544 | tf_op jit(solution)/shard_map/while/body/eval_jaxpr/ppermute | solution.py:13
  18.3 2.0 conditional.2
  25.3 5.7 %collective-permute-done = bf16[256]{0:T(256)(128)(2,1)S(1)} collective-permute-done((bf16[256]{0:T(256)(128)(2,1)S(1)}, bf16[256]{0:T(256)(128)(2,1)S(1)}, u32[]{:S(2)}, u32[]{:S(2)}) %collective-permute-start) | collective-permute-done | bytes 544 | tf_op jit(solution)/shard_map/while/body/eval_jaxpr/ppermute | solution.py:13
  32.2 2.0 conditional.2
  39.2 5.7 %collective-permute-done = bf16[256]{0:T(256)(128)(2,1)S(1)} collective-permute-done((bf16[256]{0:T(256)(128)(2,1)S(1)}, bf16[256]{0:T(256)(128)(2,1)S(1)}, u32[]{:S(2)}, u32[]{:S(2)}) %collective-permute-start) | collective-permute-done | bytes 544 | tf_op jit(solution)/shard_map/while/body/eval_jaxpr/ppermute | solution.py:13
  46.0 2.0 conditional.2
  53.0 5.7 %collective-permute-done = bf16[256]{0:T(256)(128)(2,1)S(1)} collective-permute-done((bf16[256]{0:T(256)(128)(2,1)S(1)}, bf16[256]{0:T(256)(128)(2,1)S(1)}, u32[]{:S(2)}, u32[]{:S(2)}) %collective-permute-start) | collective-permute-done | bytes 544 | tf_op jit(solution)/shard_map/while/body/eval_jaxpr/ppermute | solution.py:13
  66.9 5.7 %collective-permute-done = bf16[256]{0:T(256)(128)(2,1)S(1)} collective-permute-done((bf16[256]{0:T(256)(128)(2,1)S(1)}, bf16[256]{0:T(256)(128)(2,1)S(1)}, u32[]{:S(2)}, u32[]{:S(2)}) %collective-permute-start) | collective-permute-done | bytes 544 | tf_op jit(solution)/shard_map/while/body/eval_jaxpr/ppermute | solution.py:13
  73.7 2.0 conditional.2
  80.7 5.7 %collective-permute-done = bf16[256]{0:T(256)(128)(2,1)S(1)} collective-permute-done((bf16[256]{0:T(256)(128)(2,1)S(1)}, bf16[256]{0:T(256)(128)(2,1)S(1)}, u32[]{:S(2)}, u32[]{:S(2)}) %collective-permute-start) | collective-permute-done | bytes 544 | tf_op jit(solution)/shard_map/while/body/eval_jaxpr/ppermute | solution.py:13
  87.6 2.0 conditional.2
  94.6 5.7 %collective-permute-done = bf16[256]{0:T(256)(128)(2,1)S(1)} collective-permute-done((bf16[256]{0:T(256)(128)(2,1)S(1)}, bf16[256]{0:T(256)(128)(2,1)S(1)}, u32[]{:S(2)}, u32[]{:S(2)}) %collective-permute-start) | collective-permute-done | bytes 544 | tf_op jit(solution)/shard_map/while/body/eval_jaxpr/ppermute | solution.py:13
  101.4 2.0 conditional.2
  108.5 5.7 %collective-permute-done = bf16[256]{0:T(256)(128)(2,1)S(1)} collective-permute-done((bf16[256]{0:T(256)(128)(2,1)S(1)}, bf16[256]{0:T(256)(128)(2,1)S(1)}, u32[]{:S(2)}, u32[]{:S(2)}) %collective-permute-start) | collective-permute-done | bytes 544 | tf_op jit(solution)/shard_map/while/body/eval_jaxpr/ppermute | solution.py:13
  122.3 5.7 %collective-permute-done = bf16[256]{0:T(256)(128)(2,1)S(1)} collective-permute-done((bf16[256]{0:T(256)(128)(2,1)S(1)}, bf16[256]{0:T(256)(128)(2,1)S(1)}, u32[]{:S(2)}, u32[]{:S(2)}) %collective-permute-start) | collective-permute-done | bytes 544 | tf_op jit(solution)/shard_map/while/body/eval_jaxpr/ppermute | solution.py:13
  129.2 2.0 conditional.2
  136.2 5.8 %collective-permute-done = bf16[256]{0:T(256)(128)(2,1)S(1)} collective-permute-done((bf16[256]{0:T(256)(128)(2,1)S(1)}, bf16[256]{0:T(256)(128)(2,1)S(1)}, u32[]{:S(2)}, u32[]{:S(2)}) %collective-permute-start) | collective-permute-done | bytes 544 | tf_op jit(solution)/shard_map/while/body/eval_jaxpr/ppermute | solution.py:13
  143.1 2.0 conditional.2
  150.1 6.4 %collective-permute-done = bf16[256]{0:T(256)(128)(2,1)S(1)} collective-permute-done((bf16[256]{0:T(256)(128)(2,1)S(1)}, bf16[256]{0:T(256)(128)(2,1)S(1)}, u32[]{:S(2)}, u32[]{:S(2)}) %collective-permute-start) | collective-permute-done | bytes 544 | tf_op jit(solution)/shard_map/while/body/eval_jaxpr/ppermute | solution.py:13
  157.7 2.0 conditional.2
  164.7 5.7 %collective-permute-done = bf16[256]{0:T(256)(128)(2,1)S(1)} collective-permute-done((bf16[256]{0:T(256)(128)(2,1)S(1)}, bf16[256]{0:T(256)(128)(2,1)S(1)}, u32[]{:S(2)}, u32[]{:S(2)}) %collective-permute-start) | collective-permute-done | bytes 544 | tf_op jit(solution)/shard_map/while/body/eval_jaxpr/ppermute | solution.py:13
  171.6 2.0 conditional.2
  178.6 5.7 %collective-permute-done = bf16[256]{0:T(256)(128)(2,1)S(1)} collective-permute-done((bf16[256]{0:T(256)(128)(2,1)S(1)}, bf16[256]{0:T(256)(128)(2,1)S(1)}, u32[]{:S(2)}, u32[]{:S(2)}) %collective-permute-start) | collective-permute-done | bytes 544 | tf_op jit(solution)/shard_map/while/body/eval_jaxpr/ppermute | solution.py:13
  185.4 2.0 conditional.2
  192.4 5.7 %collective-permute-done = bf16[256]{0:T(256)(128)(2,1)S(1)} collective-permute-done((bf16[256]{0:T(256)(128)(2,1)S(1)}, bf16[256]{0:T(256)(128)(2,1)S(1)}, u32[]{:S(2)}, u32[]{:S(2)}) %collective-permute-start) | collective-permute-done | bytes 544 | tf_op jit(solution)/shard_map/while/body/eval_jaxpr/ppermute | solution.py:13
  199.3 1.9 conditional.2
  206.3 5.7 %collective-permute-done = bf16[256]{0:T(256)(128)(2,1)S(1)} collective-permute-done((bf16[256]{0:T(256)(128)(2,1)S(1)}, bf16[256]{0:T(256)(128)(2,1)S(1)}, u32[]{:S(2)}, u32[]{:S(2)}) %collective-permute-start) | collective-permute-done | bytes 544 | tf_op jit(solution)/shard_map/while/body/eval_jaxpr/ppermute | solution.py:13
  213.1 2.0 conditional.2
  220.1 5.7 %collective-permute-done = bf16[256]{0:T(256)(128)(2,1)S(1)} collective-permute-done((bf16[256]{0:T(256)(128)(2,1)S(1)}, bf16[256]{0:T(256)(128)(2,1)S(1)}, u32[]{:S(2)}, u32[]{:S(2)}) %collective-permute-start) | collective-permute-done | bytes 544 | tf_op jit(solution)/shard_map/while/body/eval_jaxpr/ppermute | solution.py:13
  (237 shorter events, 115.0 us)
Async XLA Ops:
  4.9 13.4 %collective-permute-start.1 = (bf16[2,256,128]{2,1,0:T(8,128)(2,1)S(1)}, bf16[2,256,128]{2,1,0:T(8,128)(2,1)S(1)}, u32[]{:S(2)}, u32[]{:S(2)}) collective-permute-start(bf16[2,256,128]{2,1,0:T(8,128)(2,1)S(1)} %get-tuple-element.215), channel_id=1, source_target_pairs={{0,8},{8,16},{16,24},{24,32},{32,40},{40,48},{48,56},{56,64},{64,7... | collective-permute-start | bytes 393224 | tf_op jit(solution)/shard_map/while/body/eval_jaxpr/ppermute | solution.py:13
  8.4 8.8 %collective-permute-start = (bf16[256]{0:T(256)(128)(2,1)S(1)}, bf16[256]{0:T(256)(128)(2,1)S(1)}, u32[]{:S(2)}, u32[]{:S(2)}) collective-permute-start(bf16[256]{0:T(256)(128)(2,1)S(1)} %get-tuple-element.216), channel_id=1, source_target_pairs={{0,8},{8,16},{16,24},{24,32},{32,40},{40,48},{48,56},{56,64},{64,7... | collective-permute-start | bytes 1544 | tf_op jit(solution)/shard_map/while/body/eval_jaxpr/ppermute | solution.py:13
  20.3 11.9 %collective-permute-start.1 = (bf16[2,256,128]{2,1,0:T(8,128)(2,1)S(1)}, bf16[2,256,128]{2,1,0:T(8,128)(2,1)S(1)}, u32[]{:S(2)}, u32[]{:S(2)}) collective-permute-start(bf16[2,256,128]{2,1,0:T(8,128)(2,1)S(1)} %get-tuple-element.215), channel_id=1, source_target_pairs={{0,8},{8,16},{16,24},{24,32},{32,40},{40,48},{48,56},{56,64},{64,7... | collective-permute-start | bytes 393224 | tf_op jit(solution)/shard_map/while/body/eval_jaxpr/ppermute | solution.py:13
  22.2 8.8 %collective-permute-start = (bf16[256]{0:T(256)(128)(2,1)S(1)}, bf16[256]{0:T(256)(128)(2,1)S(1)}, u32[]{:S(2)}, u32[]{:S(2)}) collective-permute-start(bf16[256]{0:T(256)(128)(2,1)S(1)} %get-tuple-element.216), channel_id=1, source_target_pairs={{0,8},{8,16},{16,24},{24,32},{32,40},{40,48},{48,56},{56,64},{64,7... | collective-permute-start | bytes 1544 | tf_op jit(solution)/shard_map/while/body/eval_jaxpr/ppermute | solution.py:13
  34.2 11.9 %collective-permute-start.1 = (bf16[2,256,128]{2,1,0:T(8,128)(2,1)S(1)}, bf16[2,256,128]{2,1,0:T(8,128)(2,1)S(1)}, u32[]{:S(2)}, u32[]{:S(2)}) collective-permute-start(bf16[2,256,128]{2,1,0:T(8,128)(2,1)S(1)} %get-tuple-element.215), channel_id=1, source_target_pairs={{0,8},{8,16},{16,24},{24,32},{32,40},{40,48},{48,56},{56,64},{64,7... | collective-permute-start | bytes 393224 | tf_op jit(solution)/shard_map/while/body/eval_jaxpr/ppermute | solution.py:13
  36.1 8.8 %collective-permute-start = (bf16[256]{0:T(256)(128)(2,1)S(1)}, bf16[256]{0:T(256)(128)(2,1)S(1)}, u32[]{:S(2)}, u32[]{:S(2)}) collective-permute-start(bf16[256]{0:T(256)(128)(2,1)S(1)} %get-tuple-element.216), channel_id=1, source_target_pairs={{0,8},{8,16},{16,24},{24,32},{32,40},{40,48},{48,56},{56,64},{64,7... | collective-permute-start | bytes 1544 | tf_op jit(solution)/shard_map/while/body/eval_jaxpr/ppermute | solution.py:13
  48.0 11.9 %collective-permute-start.1 = (bf16[2,256,128]{2,1,0:T(8,128)(2,1)S(1)}, bf16[2,256,128]{2,1,0:T(8,128)(2,1)S(1)}, u32[]{:S(2)}, u32[]{:S(2)}) collective-permute-start(bf16[2,256,128]{2,1,0:T(8,128)(2,1)S(1)} %get-tuple-element.215), channel_id=1, source_target_pairs={{0,8},{8,16},{16,24},{24,32},{32,40},{40,48},{48,56},{56,64},{64,7... | collective-permute-start | bytes 393224 | tf_op jit(solution)/shard_map/while/body/eval_jaxpr/ppermute | solution.py:13
  49.9 8.8 %collective-permute-start = (bf16[256]{0:T(256)(128)(2,1)S(1)}, bf16[256]{0:T(256)(128)(2,1)S(1)}, u32[]{:S(2)}, u32[]{:S(2)}) collective-permute-start(bf16[256]{0:T(256)(128)(2,1)S(1)} %get-tuple-element.216), channel_id=1, source_target_pairs={{0,8},{8,16},{16,24},{24,32},{32,40},{40,48},{48,56},{56,64},{64,7... | collective-permute-start | bytes 1544 | tf_op jit(solution)/shard_map/while/body/eval_jaxpr/ppermute | solution.py:13
  61.9 11.9 %collective-permute-start.1 = (bf16[2,256,128]{2,1,0:T(8,128)(2,1)S(1)}, bf16[2,256,128]{2,1,0:T(8,128)(2,1)S(1)}, u32[]{:S(2)}, u32[]{:S(2)}) collective-permute-start(bf16[2,256,128]{2,1,0:T(8,128)(2,1)S(1)} %get-tuple-element.215), channel_id=1, source_target_pairs={{0,8},{8,16},{16,24},{24,32},{32,40},{40,48},{48,56},{56,64},{64,7... | collective-permute-start | bytes 393224 | tf_op jit(solution)/shard_map/while/body/eval_jaxpr/ppermute | solution.py:13
  63.8 8.8 %collective-permute-start = (bf16[256]{0:T(256)(128)(2,1)S(1)}, bf16[256]{0:T(256)(128)(2,1)S(1)}, u32[]{:S(2)}, u32[]{:S(2)}) collective-permute-start(bf16[256]{0:T(256)(128)(2,1)S(1)} %get-tuple-element.216), channel_id=1, source_target_pairs={{0,8},{8,16},{16,24},{24,32},{32,40},{40,48},{48,56},{56,64},{64,7... | collective-permute-start | bytes 1544 | tf_op jit(solution)/shard_map/while/body/eval_jaxpr/ppermute | solution.py:13
  75.7 11.9 %collective-permute-start.1 = (bf16[2,256,128]{2,1,0:T(8,128)(2,1)S(1)}, bf16[2,256,128]{2,1,0:T(8,128)(2,1)S(1)}, u32[]{:S(2)}, u32[]{:S(2)}) collective-permute-start(bf16[2,256,128]{2,1,0:T(8,128)(2,1)S(1)} %get-tuple-element.215), channel_id=1, source_target_pairs={{0,8},{8,16},{16,24},{24,32},{32,40},{40,48},{48,56},{56,64},{64,7... | collective-permute-start | bytes 393224 | tf_op jit(solution)/shard_map/while/body/eval_jaxpr/ppermute | solution.py:13
  77.7 8.8 %collective-permute-start = (bf16[256]{0:T(256)(128)(2,1)S(1)}, bf16[256]{0:T(256)(128)(2,1)S(1)}, u32[]{:S(2)}, u32[]{:S(2)}) collective-permute-start(bf16[256]{0:T(256)(128)(2,1)S(1)} %get-tuple-element.216), channel_id=1, source_target_pairs={{0,8},{8,16},{16,24},{24,32},{32,40},{40,48},{48,56},{56,64},{64,7... | collective-permute-start | bytes 1544 | tf_op jit(solution)/shard_map/while/body/eval_jaxpr/ppermute | solution.py:13
  89.6 11.9 %collective-permute-start.1 = (bf16[2,256,128]{2,1,0:T(8,128)(2,1)S(1)}, bf16[2,256,128]{2,1,0:T(8,128)(2,1)S(1)}, u32[]{:S(2)}, u32[]{:S(2)}) collective-permute-start(bf16[2,256,128]{2,1,0:T(8,128)(2,1)S(1)} %get-tuple-element.215), channel_id=1, source_target_pairs={{0,8},{8,16},{16,24},{24,32},{32,40},{40,48},{48,56},{56,64},{64,7... | collective-permute-start | bytes 393224 | tf_op jit(solution)/shard_map/while/body/eval_jaxpr/ppermute | solution.py:13
  91.5 8.8 %collective-permute-start = (bf16[256]{0:T(256)(128)(2,1)S(1)}, bf16[256]{0:T(256)(128)(2,1)S(1)}, u32[]{:S(2)}, u32[]{:S(2)}) collective-permute-start(bf16[256]{0:T(256)(128)(2,1)S(1)} %get-tuple-element.216), channel_id=1, source_target_pairs={{0,8},{8,16},{16,24},{24,32},{32,40},{40,48},{48,56},{56,64},{64,7... | collective-permute-start | bytes 1544 | tf_op jit(solution)/shard_map/while/body/eval_jaxpr/ppermute | solution.py:13
  103.4 11.9 %collective-permute-start.1 = (bf16[2,256,128]{2,1,0:T(8,128)(2,1)S(1)}, bf16[2,256,128]{2,1,0:T(8,128)(2,1)S(1)}, u32[]{:S(2)}, u32[]{:S(2)}) collective-permute-start(bf16[2,256,128]{2,1,0:T(8,128)(2,1)S(1)} %get-tuple-element.215), channel_id=1, source_target_pairs={{0,8},{8,16},{16,24},{24,32},{32,40},{40,48},{48,56},{56,64},{64,7... | collective-permute-start | bytes 393224 | tf_op jit(solution)/shard_map/while/body/eval_jaxpr/ppermute | solution.py:13
  105.4 8.8 %collective-permute-start = (bf16[256]{0:T(256)(128)(2,1)S(1)}, bf16[256]{0:T(256)(128)(2,1)S(1)}, u32[]{:S(2)}, u32[]{:S(2)}) collective-permute-start(bf16[256]{0:T(256)(128)(2,1)S(1)} %get-tuple-element.216), channel_id=1, source_target_pairs={{0,8},{8,16},{16,24},{24,32},{32,40},{40,48},{48,56},{56,64},{64,7... | collective-permute-start | bytes 1544 | tf_op jit(solution)/shard_map/while/body/eval_jaxpr/ppermute | solution.py:13
  117.3 11.9 %collective-permute-start.1 = (bf16[2,256,128]{2,1,0:T(8,128)(2,1)S(1)}, bf16[2,256,128]{2,1,0:T(8,128)(2,1)S(1)}, u32[]{:S(2)}, u32[]{:S(2)}) collective-permute-start(bf16[2,256,128]{2,1,0:T(8,128)(2,1)S(1)} %get-tuple-element.215), channel_id=1, source_target_pairs={{0,8},{8,16},{16,24},{24,32},{32,40},{40,48},{48,56},{56,64},{64,7... | collective-permute-start | bytes 393224 | tf_op jit(solution)/shard_map/while/body/eval_jaxpr/ppermute | solution.py:13
  119.2 8.8 %collective-permute-start = (bf16[256]{0:T(256)(128)(2,1)S(1)}, bf16[256]{0:T(256)(128)(2,1)S(1)}, u32[]{:S(2)}, u32[]{:S(2)}) collective-permute-start(bf16[256]{0:T(256)(128)(2,1)S(1)} %get-tuple-element.216), channel_id=1, source_target_pairs={{0,8},{8,16},{16,24},{24,32},{32,40},{40,48},{48,56},{56,64},{64,7... | collective-permute-start | bytes 1544 | tf_op jit(solution)/shard_map/while/body/eval_jaxpr/ppermute | solution.py:13
  131.2 11.9 %collective-permute-start.1 = (bf16[2,256,128]{2,1,0:T(8,128)(2,1)S(1)}, bf16[2,256,128]{2,1,0:T(8,128)(2,1)S(1)}, u32[]{:S(2)}, u32[]{:S(2)}) collective-permute-start(bf16[2,256,128]{2,1,0:T(8,128)(2,1)S(1)} %get-tuple-element.215), channel_id=1, source_target_pairs={{0,8},{8,16},{16,24},{24,32},{32,40},{40,48},{48,56},{56,64},{64,7... | collective-permute-start | bytes 393224 | tf_op jit(solution)/shard_map/while/body/eval_jaxpr/ppermute | solution.py:13
  133.1 8.8 %collective-permute-start = (bf16[256]{0:T(256)(128)(2,1)S(1)}, bf16[256]{0:T(256)(128)(2,1)S(1)}, u32[]{:S(2)}, u32[]{:S(2)}) collective-permute-start(bf16[256]{0:T(256)(128)(2,1)S(1)} %get-tuple-element.216), channel_id=1, source_target_pairs={{0,8},{8,16},{16,24},{24,32},{32,40},{40,48},{48,56},{56,64},{64,7... | collective-permute-start | bytes 1544 | tf_op jit(solution)/shard_map/while/body/eval_jaxpr/ppermute | solution.py:13
  145.1 12.6 %collective-permute-start.1 = (bf16[2,256,128]{2,1,0:T(8,128)(2,1)S(1)}, bf16[2,256,128]{2,1,0:T(8,128)(2,1)S(1)}, u32[]{:S(2)}, u32[]{:S(2)}) collective-permute-start(bf16[2,256,128]{2,1,0:T(8,128)(2,1)S(1)} %get-tuple-element.215), channel_id=1, source_target_pairs={{0,8},{8,16},{16,24},{24,32},{32,40},{40,48},{48,56},{56,64},{64,7... | collective-permute-start | bytes 393224 | tf_op jit(solution)/shard_map/while/body/eval_jaxpr/ppermute | solution.py:13
  147.0 9.5 %collective-permute-start = (bf16[256]{0:T(256)(128)(2,1)S(1)}, bf16[256]{0:T(256)(128)(2,1)S(1)}, u32[]{:S(2)}, u32[]{:S(2)}) collective-permute-start(bf16[256]{0:T(256)(128)(2,1)S(1)} %get-tuple-element.216), channel_id=1, source_target_pairs={{0,8},{8,16},{16,24},{24,32},{32,40},{40,48},{48,56},{56,64},{64,7... | collective-permute-start | bytes 1544 | tf_op jit(solution)/shard_map/while/body/eval_jaxpr/ppermute | solution.py:13
  159.7 11.9 %collective-permute-start.1 = (bf16[2,256,128]{2,1,0:T(8,128)(2,1)S(1)}, bf16[2,256,128]{2,1,0:T(8,128)(2,1)S(1)}, u32[]{:S(2)}, u32[]{:S(2)}) collective-permute-start(bf16[2,256,128]{2,1,0:T(8,128)(2,1)S(1)} %get-tuple-element.215), channel_id=1, source_target_pairs={{0,8},{8,16},{16,24},{24,32},{32,40},{40,48},{48,56},{56,64},{64,7... | collective-permute-start | bytes 393224 | tf_op jit(solution)/shard_map/while/body/eval_jaxpr/ppermute | solution.py:13
  161.6 8.8 %collective-permute-start = (bf16[256]{0:T(256)(128)(2,1)S(1)}, bf16[256]{0:T(256)(128)(2,1)S(1)}, u32[]{:S(2)}, u32[]{:S(2)}) collective-permute-start(bf16[256]{0:T(256)(128)(2,1)S(1)} %get-tuple-element.216), channel_id=1, source_target_pairs={{0,8},{8,16},{16,24},{24,32},{32,40},{40,48},{48,56},{56,64},{64,7... | collective-permute-start | bytes 1544 | tf_op jit(solution)/shard_map/while/body/eval_jaxpr/ppermute | solution.py:13
  173.6 11.9 %collective-permute-start.1 = (bf16[2,256,128]{2,1,0:T(8,128)(2,1)S(1)}, bf16[2,256,128]{2,1,0:T(8,128)(2,1)S(1)}, u32[]{:S(2)}, u32[]{:S(2)}) collective-permute-start(bf16[2,256,128]{2,1,0:T(8,128)(2,1)S(1)} %get-tuple-element.215), channel_id=1, source_target_pairs={{0,8},{8,16},{16,24},{24,32},{32,40},{40,48},{48,56},{56,64},{64,7... | collective-permute-start | bytes 393224 | tf_op jit(solution)/shard_map/while/body/eval_jaxpr/ppermute | solution.py:13
  175.5 8.8 %collective-permute-start = (bf16[256]{0:T(256)(128)(2,1)S(1)}, bf16[256]{0:T(256)(128)(2,1)S(1)}, u32[]{:S(2)}, u32[]{:S(2)}) collective-permute-start(bf16[256]{0:T(256)(128)(2,1)S(1)} %get-tuple-element.216), channel_id=1, source_target_pairs={{0,8},{8,16},{16,24},{24,32},{32,40},{40,48},{48,56},{56,64},{64,7... | collective-permute-start | bytes 1544 | tf_op jit(solution)/shard_map/while/body/eval_jaxpr/ppermute | solution.py:13
  187.4 11.9 %collective-permute-start.1 = (bf16[2,256,128]{2,1,0:T(8,128)(2,1)S(1)}, bf16[2,256,128]{2,1,0:T(8,128)(2,1)S(1)}, u32[]{:S(2)}, u32[]{:S(2)}) collective-permute-start(bf16[2,256,128]{2,1,0:T(8,128)(2,1)S(1)} %get-tuple-element.215), channel_id=1, source_target_pairs={{0,8},{8,16},{16,24},{24,32},{32,40},{40,48},{48,56},{56,64},{64,7... | collective-permute-start | bytes 393224 | tf_op jit(solution)/shard_map/while/body/eval_jaxpr/ppermute | solution.py:13
  189.4 8.8 %collective-permute-start = (bf16[256]{0:T(256)(128)(2,1)S(1)}, bf16[256]{0:T(256)(128)(2,1)S(1)}, u32[]{:S(2)}, u32[]{:S(2)}) collective-permute-start(bf16[256]{0:T(256)(128)(2,1)S(1)} %get-tuple-element.216), channel_id=1, source_target_pairs={{0,8},{8,16},{16,24},{24,32},{32,40},{40,48},{48,56},{56,64},{64,7... | collective-permute-start | bytes 1544 | tf_op jit(solution)/shard_map/while/body/eval_jaxpr/ppermute | solution.py:13
  201.3 11.9 %collective-permute-start.1 = (bf16[2,256,128]{2,1,0:T(8,128)(2,1)S(1)}, bf16[2,256,128]{2,1,0:T(8,128)(2,1)S(1)}, u32[]{:S(2)}, u32[]{:S(2)}) collective-permute-start(bf16[2,256,128]{2,1,0:T(8,128)(2,1)S(1)} %get-tuple-element.215), channel_id=1, source_target_pairs={{0,8},{8,16},{16,24},{24,32},{32,40},{40,48},{48,56},{56,64},{64,7... | collective-permute-start | bytes 393224 | tf_op jit(solution)/shard_map/while/body/eval_jaxpr/ppermute | solution.py:13
  203.2 8.8 %collective-permute-start = (bf16[256]{0:T(256)(128)(2,1)S(1)}, bf16[256]{0:T(256)(128)(2,1)S(1)}, u32[]{:S(2)}, u32[]{:S(2)}) collective-permute-start(bf16[256]{0:T(256)(128)(2,1)S(1)} %get-tuple-element.216), channel_id=1, source_target_pairs={{0,8},{8,16},{16,24},{24,32},{32,40},{40,48},{48,56},{56,64},{64,7... | collective-permute-start | bytes 1544 | tf_op jit(solution)/shard_map/while/body/eval_jaxpr/ppermute | solution.py:13
  215.1 11.9 %collective-permute-start.1 = (bf16[2,256,128]{2,1,0:T(8,128)(2,1)S(1)}, bf16[2,256,128]{2,1,0:T(8,128)(2,1)S(1)}, u32[]{:S(2)}, u32[]{:S(2)}) collective-permute-start(bf16[2,256,128]{2,1,0:T(8,128)(2,1)S(1)} %get-tuple-element.215), channel_id=1, source_target_pairs={{0,8},{8,16},{16,24},{24,32},{32,40},{40,48},{48,56},{56,64},{64,7... | collective-permute-start | bytes 393224 | tf_op jit(solution)/shard_map/while/body/eval_jaxpr/ppermute | solution.py:13
  217.1 8.8 %collective-permute-start = (bf16[256]{0:T(256)(128)(2,1)S(1)}, bf16[256]{0:T(256)(128)(2,1)S(1)}, u32[]{:S(2)}, u32[]{:S(2)}) collective-permute-start(bf16[256]{0:T(256)(128)(2,1)S(1)} %get-tuple-element.216), channel_id=1, source_target_pairs={{0,8},{8,16},{16,24},{24,32},{32,40},{40,48},{48,56},{56,64},{64,7... | collective-permute-start | bytes 1544 | tf_op jit(solution)/shard_map/while/body/eval_jaxpr/ppermute | solution.py:13
  (2 other events, 2.1 us)
where the time goes:
time: 231 us; the launch traced here: 229 us
  waiting for transfers between devices  90.1 us (39%)
  starting transfers between devices  64.6 us (28%)
  matrix products  24.1 us (10%)
  local copies, waits for them, and re-layouts  21.4 us (9%)
  loops' own time  20.4 us (9%)
  other arithmetic  7.87 us (3%)
    ppermute x32, waiting for transfers between devices, shifted(): return lax.ppermute(x, axis, pairs)  90.1 us
    ppermute x32, starting transfers between devices, shifted(): return lax.ppermute(x, axis, pairs)  64.6 us
    another operation x1, loops' own time, on_device(): lax.scan(advance, (carried, keys_values, own_docs), jnp.arange(1, REACH +...  19.4 us
    dot_general x16, matrix products, attend_piece(): jnp.einsum('kgtn,nkd->kgtd', weights.astype(jnp.bfloat16), value_rows, pr...  15.8 us
    dynamic_slice x16, local copies, waits for them, and re-layouts, on_device(): lax.scan(advance, (carried, keys_values, own_docs), jnp.arange(1, REACH +...  9.31 us
    slice x16, local copies, waits for them, and re-layouts, far_piece(): needed = (source >= 0) & (piece_docs[tok_rows - 1] == own_docs[0])  9.22 us
    dot_general x16, matrix products, attend_piece(): jnp.einsum('tkgd,nkd->kgtn', grouped, key_rows, preferred_element_type=jn...  8.27 us
    reduce_sum x16, other arithmetic, attend_piece(): row_total = row_total * factor + jnp.sum(weights, axis=-1)  4.71 us
  transfers between devices with their start and end apart: 32, of which 16 were waited for; matrix products, arithmetic and copies ran while one was open for 8% of the time, Pallas kernels for 0%

commit v1 on v0

v1 whole, which is shorter than its diff:
```python
import functools
import itertools
import jax
import jax.numpy as jnp
from jax import lax
from jax.experimental import pallas as pl
from jax.experimental.pallas import tpu as pltpu
from jax.sharding import PartitionSpec as P

HD = 128
FAR = 1e30
FACTOR = HD ** (-0.5) * 1.4426950408889634
F32, BF16 = jnp.float32, jnp.bfloat16
NT = (((1,), (1,)), ((), ()))
YS = 4
ROUNDS = ((0, 1), (2, 3))


def pack_kernel(kv_ref, docs_ref, piece_ref, rows_ref):
    tok = kv_ref.shape[1]
    piece_ref[0:tok] = kv_ref[0]
    piece_ref[tok : 2 * tok] = kv_ref[1]
    docs = docs_ref[...].astype(F32)
    n = docs.shape[0]
    piece_ref[2 * tok :] = jnp.concatenate([docs, jnp.zeros((16 - n, HD), F32)], 0).astype(BF16)
    for t in range(n):
        rows_ref[t * HD : (t + 1) * HD] = jnp.broadcast_to(docs[t : t + 1], (HD, HD)).T


def key_docs(piece_ref, lead, tok):
    tail = piece_ref[lead + (slice(2 * tok, 2 * tok + 16),)].astype(F32)
    return jnp.concatenate([tail[t : t + 1] for t in range(tok // HD)], 1)


def own_kernel(q_ref, rows_ref, piece_ref, m_ref, l_ref, acc_ref):
    tok = q_ref.shape[0]
    keys = piece_ref[0:tok]
    values = jnp.concatenate([piece_ref[tok : 2 * tok], jnp.ones((tok, HD), BF16)], 1)
    docs = key_docs(piece_ref, (), tok)
    seen = (rows_ref[:, 0:1] == docs) & (
        lax.broadcasted_iota(jnp.int32, (tok, tok), 1) <= lax.broadcasted_iota(jnp.int32, (tok, tok), 0)
    )
    for h in range(q_ref.shape[1] // HD):
        s = lax.dot_general(q_ref[:, h * HD : (h + 1) * HD], keys, NT, preferred_element_type=F32)
        s = jnp.where(seen, s, -FAR)
        m = jnp.max(s, 1, keepdims=True)
        p = jnp.exp2((s - m) * FACTOR).astype(BF16)
        o = jnp.dot(p, values, preferred_element_type=F32)
        m_ref[h] = jnp.broadcast_to(m, (tok, HD))
        acc_ref[h] = o[:, :HD]
        l_ref[h] = o[:, HD:]


def far_kernel(last, n_refs, *refs):
    q_ref, rows_ref = refs[:2]
    piece_refs = refs[2 : 2 + n_refs]
    m_in, l_in, acc_in = refs[2 + n_refs : 5 + n_refs]
    outs = refs[5 + n_refs : -2]
    s_ref, mx_ref = refs[-2:]
    tok = q_ref.shape[0]
    heads = q_ref.shape[1] // HD
    pieces = [(r, i) for r in piece_refs for i in itertools.product(*[range(s) for s in r.shape[:-2]])]
    first = rows_ref[0:1, 0:1]
    row_off = jnp.where(rows_ref[...] == first, 0.0, FAR)
    bias = [jnp.where(key_docs(r, i, tok) == first, 0.0, -FAR) for r, i in pieces]

    def score(h, slot):
        q = q_ref[:, pl.ds(pl.multiple_of(h * HD, HD), HD)]
        mx = None
        for k, (r, i) in enumerate(pieces):
            s = lax.dot_general(q, r[i + (slice(0, tok),)], NT, preferred_element_type=F32) + bias[k]
            s_ref[slot, :, k * tok : (k + 1) * tok] = s
            for t in range(tok // HD):
                part = s[:, t * HD : (t + 1) * HD]
                mx = part if mx is None else jnp.maximum(mx, part)
        mx_ref[slot] = mx

    def finish(h, slot):
        m_old = m_in[h]
        m_new = jnp.maximum(m_old, jnp.max(mx_ref[slot], 1, keepdims=True) - row_off)
        alpha = jnp.exp2((m_old - m_new) * FACTOR)
        shift = jnp.concatenate([m_new + row_off] * (tok // HD), 1) * FACTOR
        o = None
        for k, (r, i) in enumerate(pieces):
            s = s_ref[slot, :, k * tok : (k + 1) * tok]
            p = jnp.exp2(s * FACTOR - shift).astype(BF16)
            v = jnp.concatenate([r[i + (slice(tok, 2 * tok),)], jnp.ones((tok, HD), BF16)], 1)
            d = jnp.dot(p, v, preferred_element_type=F32)
            o = d if o is None else o + d
        acc = acc_in[h] * alpha + o[:, :HD]
        total = l_in[h] * alpha + o[:, HD:]
        if last:
            outs[0][:, pl.ds(pl.multiple_of(h * HD, HD), HD)] = (acc / total).astype(BF16)
        else:
            outs[0][h] = m_new
            outs[1][h] = total
            outs[2][h] = acc

    score(0, 0)

    def step(h, _):
        score(jnp.minimum(h + 1, heads - 1), (h + 1) % 2)
        finish(h, h % 2)
        return 0

    lax.fori_loop(0, heads, step, 0)


def lay_kernel(count, *refs):
    levels, out = refs[:-1], refs[-1]
    y = lax.axis_index("ctx") % YS
    for slot in range(YS):
        for k in range(count):

            @pl.when(slot > y)
            def _():
                out[slot, k] = levels[k][...]

            @pl.when(slot <= y)
            def _():
                out[slot, k] = levels[k + 1][...]


VM = pl.BlockSpec(memory_space=pltpu.VMEM)


def params():
    return pltpu.CompilerParams(vmem_limit_bytes=40 * 2**20)


def pack(kv, docs):
    tok = kv.shape[1]
    return pl.pallas_call(
        pack_kernel,
        in_specs=[VM, VM],
        out_specs=[VM, VM],
        out_shape=[jax.ShapeDtypeStruct((2 * tok + 16, HD), BF16), jax.ShapeDtypeStruct((tok, HD), F32)],
        compiler_params=params(),
        name="pack",
    )(kv, docs)


def carry_shapes(q):
    heads, tok = q.shape[1] // HD, q.shape[0]
    return [jax.ShapeDtypeStruct((heads, tok, HD), F32)] * 3


def cost(rows, keys):
    return pl.CostEstimate(flops=4 * rows * keys * HD, bytes_accessed=4 * rows * HD, transcendentals=rows * keys)


def own(q, rows, piece):
    return pl.pallas_call(
        own_kernel,
        in_specs=[VM] * 3,
        out_specs=[VM] * 3,
        out_shape=carry_shapes(q),
        compiler_params=params(),
        cost_estimate=cost(q.size // HD, q.shape[0]),
        name="own",
    )(q, rows, piece)


def far(q, rows, pieces, carry, last):
    tok = q.shape[0]
    n = sum(p.size // (p.shape[-1] * p.shape[-2]) for p in pieces)
    return pl.pallas_call(
        functools.partial(far_kernel, last, len(pieces)),
        in_specs=[VM] * (5 + len(pieces)),
        out_specs=VM if last else [VM] * 3,
        out_shape=jax.ShapeDtypeStruct(q.shape, BF16) if last else carry_shapes(q),
        scratch_shapes=[pltpu.VMEM((2, tok, n * tok), F32), pltpu.VMEM((2, tok, HD), F32)],
        compiler_params=params(),
        cost_estimate=cost(q.size // HD, n * tok),
        name="far",
    )(q, rows, *pieces, *carry)


def lay(levels):
    count = len(levels) - 1
    return pl.pallas_call(
        functools.partial(lay_kernel, count),
        in_specs=[VM] * len(levels),
        out_specs=VM,
        out_shape=jax.ShapeDtypeStruct((YS, count, *levels[0].shape), BF16),
        compiler_params=params(),
        name="lay",
    )(*levels)


def on_device(queries, keys_values, segments):
    size = lax.axis_size("ctx")
    up = [(c, (c + YS) % size) for c in range(size)]
    groups = [list(range(c, c + YS)) for c in range(0, size, YS)]
    piece, rows = pack(keys_values, segments.reshape(-1, HD))
    levels = [piece]
    for _ in range(ROUNDS[-1][-1] + 1):
        levels.append(lax.ppermute(levels[-1], "ctx", up))
    carry = own(queries, rows, piece)
    for wanted in ROUNDS:
        sent = lay(levels[wanted[0] : wanted[-1] + 2])
        got = lax.all_to_all(sent, "ctx", 0, 0, axis_index_groups=groups)
        carry = far(queries, rows, [got], carry, wanted is ROUNDS[-1])
    return carry


def solution(mesh):
    return jax.shard_map(
        on_device,
        mesh=mesh,
        in_specs=(P("ctx", "tp"), P(None, "ctx", "tp"), P("ctx")),
        out_specs=P("ctx", "tp"),
        check_vma=False,
    )
```

time: 231 us -> 85.8 us (0.37)
  the two profiles are of different devices: /device:TPU:128 before, /device:TPU:12 now
where the time goes in v1:
time: 85.8 us; the launch traced here: 85.3 us
  waiting for transfers between devices  29.7 us (35%)
  Pallas kernels  27.9 us (33%)
  starting transfers between devices  19.4 us (23%)
  local copies, waits for them, and re-layouts  8.18 us (10%)
    ppermute x4, waiting for transfers between devices, on_device(): levels.append(lax.ppermute(levels[-1], 'ctx', up))  29.7 us
    pallas_call x2, Pallas kernels, far(): pl.pallas_call(functools.partial(far_kernel, last, len(pieces)), in_specs...  24.6 us
    all_to_all x2, starting transfers between devices, on_device(): got = lax.all_to_all(sent, 'ctx', 0, 0, axis_index_groups=groups)  9.84 us
    ppermute x4, starting transfers between devices, on_device(): levels.append(lax.ppermute(levels[-1], 'ctx', up))  9.55 us
    unnamed x18, local copies, waits for them, and re-layouts  8.18 us
    pallas_call x2, Pallas kernels, lay(): pl.pallas_call(functools.partial(lay_kernel, count), in_specs=[VM] * len(...  2.19 us
  transfers between devices with their start and end apart: 6, of which 4 were waited for; matrix products, arithmetic and copies ran while one was open for 0% of the time, Pallas kernels for 16%

profile of v1, /device:TPU:12, one launch (start us, length us, event | category | flops | bytes accessed | tf_op | source)
XLA Modules:
  0.0 85.3 jit_solution(5775302252884851976)
XLA Ops:
  0.0 0.0 copy-start
  0.0 0.9 %copy-done = bf16[2,256,128]{2,1,0:T(8,128)(2,1)S(1)} copy-done((bf16[2,256,128]{2,1,0:T(8,128)(2,1)S(1)}, bf16[2,256,128]{2,1,0:T(8,128)(2,1)}, u32[]{:S(2)}) %copy-start) | copy-done | bytes 131096
  0.9 0.0 copy-start.1
  0.9 0.7 copy-done.1
  1.6 0.1 pack.1
  1.7 3.8 %collective-permute-start = (bf16[528,128]{1,0:T(8,128)(2,1)S(1)}, bf16[528,128]{1,0:T(8,128)(2,1)S(1)}, u32[]{:S(2)}, u32[]{:S(2)}) collective-permute-start(bf16[528,128]{1,0:T(8,128)(2,1)S(1)} %get-tuple-element.14.refs_0_.piece_ref), channel_id=1, source_target_pairs={{0,32},{8,40},{16,48},{24,56},{32,64},{40,72},{48,80},{56,88},{64,... | collective-permute-start | bytes 405512 | tf_op jit(solution)/shard_map/ppermute | solution.py:198
  5.5 11.1 %collective-permute-done.refs_1_ = bf16[528,128]{1,0:T(8,128)(2,1)S(1)} collective-permute-done((bf16[528,128]{1,0:T(8,128)(2,1)S(1)}, bf16[528,128]{1,0:T(8,128)(2,1)S(1)}, u32[]{:S(2)}, u32[]{:S(2)}) %collective-permute-start) | collective-permute-done | bytes 135200 | tf_op jit(solution)/shard_map/ppermute | solution.py:198
  16.7 1.9 %collective-permute-start.1 = (bf16[528,128]{1,0:T(8,128)(2,1)S(1)}, bf16[528,128]{1,0:T(8,128)(2,1)S(1)}, u32[]{:S(2)}, u32[]{:S(2)}) collective-permute-start(bf16[528,128]{1,0:T(8,128)(2,1)S(1)} %collective-permute-done.refs_1_), channel_id=1, source_target_pairs={{0,32},{8,40},{16,48},{24,56},{32,64},{40,72},{48,80},{56,88},{64,... | collective-permute-start | bytes 405512 | tf_op jit(solution)/shard_map/ppermute | solution.py:198
  18.6 6.2 %collective-permute-done.1.refs_0_.refs_2_ = bf16[528,128]{1,0:T(8,128)(2,1)S(1)} collective-permute-done((bf16[528,128]{1,0:T(8,128)(2,1)S(1)}, bf16[528,128]{1,0:T(8,128)(2,1)S(1)}, u32[]{:S(2)}, u32[]{:S(2)}) %collective-permute-start.1) | collective-permute-done | bytes 135200 | tf_op jit(solution)/shard_map/ppermute | solution.py:198
  24.8 1.1 %lay.3 = bf16[4,2,528,128]{3,2,1,0:T(8,128)(2,1)} custom-call(bf16[528,128]{1,0:T(8,128)(2,1)S(1)} %get-tuple-element.14.refs_0_.piece_ref, bf16[528,128]{1,0:T(8,128)(2,1)S(1)} %collective-permute-done.refs_1_, bf16[528,128]{1,0:T(8,128)(2,1)S(1)} %collective-permute-done.1.refs_0_.refs_2_), custom_call_target="tpu_custom_call" | custom-call | tf_op jit(solution)/shard_map/lay/pallas_call | solution.py:181
  25.9 4.9 %all-to-all-start.1 = ((bf16[4,2,528,128]{3,2,1,0:T(8,128)(2,1)}), bf16[4,2,528,128]{3,2,1,0:T(8,128)(2,1)S(1)}, u32[]{:S(2)}, u32[]{:S(2)}) async-start(bf16[4,2,528,128]{3,2,1,0:T(8,128)(2,1)} %lay.3), calls=%async_computation.1 | async-start | bytes 2162688 | tf_op jit(solution)/shard_map/all_to_all | solution.py:202
  30.8 1.9 %collective-permute-start.2 = (bf16[528,128]{1,0:T(8,128)(2,1)S(1)}, bf16[528,128]{1,0:T(8,128)(2,1)S(1)}, u32[]{:S(2)}, u32[]{:S(2)}) collective-permute-start(bf16[528,128]{1,0:T(8,128)(2,1)S(1)} %collective-permute-done.1.refs_0_.refs_2_), channel_id=1, source_target_pairs={{0,32},{8,40},{16,48},{24,56},{32,64},{40,72},{48,80},{56,88},{64,... | collective-permute-start | bytes 405512 | tf_op jit(solution)/shard_map/ppermute | solution.py:198
  32.7 6.2 %collective-permute-done.2.refs_1_ = bf16[528,128]{1,0:T(8,128)(2,1)S(1)} collective-permute-done((bf16[528,128]{1,0:T(8,128)(2,1)S(1)}, bf16[528,128]{1,0:T(8,128)(2,1)S(1)}, u32[]{:S(2)}, u32[]{:S(2)}) %collective-permute-start.2) | collective-permute-done | bytes 135200 | tf_op jit(solution)/shard_map/ppermute | solution.py:198
  38.9 1.9 %collective-permute-start.3 = (bf16[528,128]{1,0:T(8,128)(2,1)S(1)}, bf16[528,128]{1,0:T(8,128)(2,1)S(1)}, u32[]{:S(2)}, u32[]{:S(2)}) collective-permute-start(bf16[528,128]{1,0:T(8,128)(2,1)S(1)} %collective-permute-done.2.refs_1_), channel_id=1, source_target_pairs={{0,32},{8,40},{16,48},{24,56},{32,64},{40,72},{48,80},{56,88},{64,... | collective-permute-start | bytes 405512 | tf_op jit(solution)/shard_map/ppermute | solution.py:198
  40.8 6.2 %collective-permute-done.3.refs_2_ = bf16[528,128]{1,0:T(8,128)(2,1)S(1)} collective-permute-done((bf16[528,128]{1,0:T(8,128)(2,1)S(1)}, bf16[528,128]{1,0:T(8,128)(2,1)S(1)}, u32[]{:S(2)}, u32[]{:S(2)}) %collective-permute-start.3) | collective-permute-done | bytes 135200 | tf_op jit(solution)/shard_map/ppermute | solution.py:198
  47.0 1.1 %lay.2 = bf16[4,2,528,128]{3,2,1,0:T(8,128)(2,1)} custom-call(bf16[528,128]{1,0:T(8,128)(2,1)S(1)} %collective-permute-done.1.refs_0_.refs_2_, bf16[528,128]{1,0:T(8,128)(2,1)S(1)} %collective-permute-done.2.refs_1_, bf16[528,128]{1,0:T(8,128)(2,1)S(1)} %collective-permute-done.3.refs_2_), custom_call_target="tpu_custom_call" | custom-call | tf_op jit(solution)/shard_map/lay/pallas_call | solution.py:181
  48.1 0.0 copy-start.2
  48.1 0.0 all-to-all-done.1.refs_2_
  48.1 4.9 %all-to-all-start = ((bf16[4,2,528,128]{3,2,1,0:T(8,128)(2,1)}), bf16[4,2,528,128]{3,2,1,0:T(8,128)(2,1)S(1)}, u32[]{:S(2)}, u32[]{:S(2)}) async-start(bf16[4,2,528,128]{3,2,1,0:T(8,128)(2,1)} %lay.2), calls=%async_computation | async-start | bytes 2162688 | tf_op jit(solution)/shard_map/all_to_all | solution.py:202
  53.0 0.0 copy-done.2
  53.0 1.0 %own.1 = (f32[8,256,128]{2,1,0:T(8,128)S(1)}, f32[8,256,128]{2,1,0:T(8,128)S(1)}, f32[8,256,128]{2,1,0:T(8,128)S(1)}) custom-call(bf16[256,1024]{1,0:T(8,128)(2,1)S(1)} %copy-done.2, f32[256,128]{1,0:T(8,128)S(1)} %get-tuple-element.13.rows_ref.refs_1_, bf16[528,128]{1,0:T(8,128)(2,1)S(1)} %get-tuple-element.14.refs_0_.piece_ref), custom_call_target="tpu_custom_call" | custom-call | flops 268435456 | bytes 1048576 | tf_op jit(solution)/shard_map/own/pallas_call | solution.py:153
  54.0 11.9 %far.2 = (f32[8,256,128]{2,1,0:T(8,128)S(1)}, f32[8,256,128]{2,1,0:T(8,128)S(1)}, f32[8,256,128]{2,1,0:T(8,128)S(1)}) custom-call(bf16[256,1024]{1,0:T(8,128)(2,1)S(1)} %copy-done.2, f32[256,128]{1,0:T(8,128)S(1)} %get-tuple-element.13.rows_ref.refs_1_, bf16[4,2,528,128]{3,2,1,0:T(8,128)(2,1)S(1)} %all-to-all-done.1.refs_2_, ...), custom_call_target="tpu_custom_call" | custom-call | flops 2147483648 | bytes 1048576 | tf_op jit(solution)/shard_map/far/pallas_call | solution.py:167
  65.9 0.0 copy-start.3
  65.9 1.0 %copy-done.3 = f32[8,256,128]{2,1,0:T(8,128)} copy-done((f32[8,256,128]{2,1,0:T(8,128)}, f32[8,256,128]{2,1,0:T(8,128)S(1)}, u32[]{:S(2)}) %copy-start.3) | copy-done | bytes 1048600
  66.9 0.0 copy-start.5
  66.9 1.0 %copy-done.5 = f32[8,256,128]{2,1,0:T(8,128)} copy-done((f32[8,256,128]{2,1,0:T(8,128)}, f32[8,256,128]{2,1,0:T(8,128)S(1)}, u32[]{:S(2)}) %copy-start.5) | copy-done | bytes 1048600
  67.9 1.0 %copy-done.7 = f32[8,256,128]{2,1,0:T(8,128)} copy-done((f32[8,256,128]{2,1,0:T(8,128)}, f32[8,256,128]{2,1,0:T(8,128)S(1)}, u32[]{:S(2)}) %copy-start.7) | copy-done | bytes 1048600
  68.8 0.0 all-to-all-done.refs_2_
  68.8 1.2 %copy-done.4 = f32[8,256,128]{2,1,0:T(8,128)S(1)} copy-done((f32[8,256,128]{2,1,0:T(8,128)S(1)}, f32[8,256,128]{2,1,0:T(8,128)}, u32[]{:S(2)}) %copy-start.4) | copy-done | bytes 1048600
  70.1 1.2 %copy-done.6 = f32[8,256,128]{2,1,0:T(8,128)S(1)} copy-done((f32[8,256,128]{2,1,0:T(8,128)S(1)}, f32[8,256,128]{2,1,0:T(8,128)}, u32[]{:S(2)}) %copy-start.6) | copy-done | bytes 1048600
  71.3 1.2 %copy-done.8 = f32[8,256,128]{2,1,0:T(8,128)S(1)} copy-done((f32[8,256,128]{2,1,0:T(8,128)S(1)}, f32[8,256,128]{2,1,0:T(8,128)}, u32[]{:S(2)}) %copy-start.8) | copy-done | bytes 1048600
  72.5 12.7 %far.3 = bf16[256,1024]{1,0:T(8,128)(2,1)} custom-call(bf16[256,1024]{1,0:T(8,128)(2,1)S(1)} %copy-done.2, f32[256,128]{1,0:T(8,128)S(1)} %get-tuple-element.13.rows_ref.refs_1_, bf16[4,2,528,128]{3,2,1,0:T(8,128)(2,1)S(1)} %all-to-all-done.refs_2_, f32[8,256,128]{2,1,0:T(8,128)S(1)} %copy-done.4, f32[8,256,128]{2,1,0:T(8,128)S(1)} %copy-done.6, ...), custom_call_target="tpu_custom_call" | custom-call | flops 2147483648 | bytes 1048576 | tf_op jit(solution)/shard_map/far/pallas_call | solution.py:167
  (4 shorter events, 0.0 us)
Async XLA Ops:
  0.0 0.9 %copy-start = (bf16[2,256,128]{2,1,0:T(8,128)(2,1)S(1)}, bf16[2,256,128]{2,1,0:T(8,128)(2,1)}, u32[]{:S(2)}) copy-start(bf16[2,256,128]{2,1,0:T(8,128)(2,1)} %kv_ref.1) | copy-start | bytes 393220
  0.9 0.7 copy-start.1
  1.7 15.0 %collective-permute-start = (bf16[528,128]{1,0:T(8,128)(2,1)S(1)}, bf16[528,128]{1,0:T(8,128)(2,1)S(1)}, u32[]{:S(2)}, u32[]{:S(2)}) collective-permute-start(bf16[528,128]{1,0:T(8,128)(2,1)S(1)} %get-tuple-element.14.refs_0_.piece_ref), channel_id=1, source_target_pairs={{0,32},{8,40},{16,48},{24,56},{32,64},{40,72},{48,80},{56,88},{64,... | collective-permute-start | bytes 405512 | tf_op jit(solution)/shard_map/ppermute | solution.py:198
  16.7 8.1 %collective-permute-start.1 = (bf16[528,128]{1,0:T(8,128)(2,1)S(1)}, bf16[528,128]{1,0:T(8,128)(2,1)S(1)}, u32[]{:S(2)}, u32[]{:S(2)}) collective-permute-start(bf16[528,128]{1,0:T(8,128)(2,1)S(1)} %collective-permute-done.refs_1_), channel_id=1, source_target_pairs={{0,32},{8,40},{16,48},{24,56},{32,64},{40,72},{48,80},{56,88},{64,... | collective-permute-start | bytes 405512 | tf_op jit(solution)/shard_map/ppermute | solution.py:198
  25.9 22.2 %all-to-all-start.1 = ((bf16[4,2,528,128]{3,2,1,0:T(8,128)(2,1)}), bf16[4,2,528,128]{3,2,1,0:T(8,128)(2,1)S(1)}, u32[]{:S(2)}, u32[]{:S(2)}) async-start(bf16[4,2,528,128]{3,2,1,0:T(8,128)(2,1)} %lay.3), calls=%async_computation.1 | async-start | bytes 2162688 | tf_op jit(solution)/shard_map/all_to_all | solution.py:202
  30.8 8.1 %collective-permute-start.2 = (bf16[528,128]{1,0:T(8,128)(2,1)S(1)}, bf16[528,128]{1,0:T(8,128)(2,1)S(1)}, u32[]{:S(2)}, u32[]{:S(2)}) collective-permute-start(bf16[528,128]{1,0:T(8,128)(2,1)S(1)} %collective-permute-done.1.refs_0_.refs_2_), channel_id=1, source_target_pairs={{0,32},{8,40},{16,48},{24,56},{32,64},{40,72},{48,80},{56,88},{64,... | collective-permute-start | bytes 405512 | tf_op jit(solution)/shard_map/ppermute | solution.py:198
  38.9 8.1 %collective-permute-start.3 = (bf16[528,128]{1,0:T(8,128)(2,1)S(1)}, bf16[528,128]{1,0:T(8,128)(2,1)S(1)}, u32[]{:S(2)}, u32[]{:S(2)}) collective-permute-start(bf16[528,128]{1,0:T(8,128)(2,1)S(1)} %collective-permute-done.2.refs_1_), channel_id=1, source_target_pairs={{0,32},{8,40},{16,48},{24,56},{32,64},{40,72},{48,80},{56,88},{64,... | collective-permute-start | bytes 405512 | tf_op jit(solution)/shard_map/ppermute | solution.py:198
  48.1 4.9 %copy-start.2 = (bf16[256,1024]{1,0:T(8,128)(2,1)S(1)}, bf16[256,1024]{1,0:T(8,128)(2,1)}, u32[]{:S(2)}) copy-start(bf16[256,1024]{1,0:T(8,128)(2,1)} %refs_0_.3) | copy-start | bytes 1572868
  48.1 20.8 %all-to-all-start = ((bf16[4,2,528,128]{3,2,1,0:T(8,128)(2,1)}), bf16[4,2,528,128]{3,2,1,0:T(8,128)(2,1)S(1)}, u32[]{:S(2)}, u32[]{:S(2)}) async-start(bf16[4,2,528,128]{3,2,1,0:T(8,128)(2,1)} %lay.2), calls=%async_computation | async-start | bytes 2162688 | tf_op jit(solution)/shard_map/all_to_all | solution.py:202
  65.9 1.0 %copy-start.3 = (f32[8,256,128]{2,1,0:T(8,128)}, f32[8,256,128]{2,1,0:T(8,128)S(1)}, u32[]{:S(2)}) copy-start(f32[8,256,128]{2,1,0:T(8,128)S(1)} %get-tuple-element.18.refs_3_) | copy-start | bytes 3145732
  66.9 1.0 %copy-start.5 = (f32[8,256,128]{2,1,0:T(8,128)}, f32[8,256,128]{2,1,0:T(8,128)S(1)}, u32[]{:S(2)}) copy-start(f32[8,256,128]{2,1,0:T(8,128)S(1)} %get-tuple-element.19.refs_4_) | copy-start | bytes 3145732
  67.9 1.0 %copy-start.7 = (f32[8,256,128]{2,1,0:T(8,128)}, f32[8,256,128]{2,1,0:T(8,128)S(1)}, u32[]{:S(2)}) copy-start(f32[8,256,128]{2,1,0:T(8,128)S(1)} %get-tuple-element.20.refs_5_) | copy-start | bytes 3145732
  68.8 1.2 %copy-start.4 = (f32[8,256,128]{2,1,0:T(8,128)S(1)}, f32[8,256,128]{2,1,0:T(8,128)}, u32[]{:S(2)}) copy-start(f32[8,256,128]{2,1,0:T(8,128)} %copy-done.3) | copy-start | bytes 3145732
  70.1 1.2 %copy-start.6 = (f32[8,256,128]{2,1,0:T(8,128)S(1)}, f32[8,256,128]{2,1,0:T(8,128)}, u32[]{:S(2)}) copy-start(f32[8,256,128]{2,1,0:T(8,128)} %copy-done.5) | copy-start | bytes 3145732
  71.3 1.2 %copy-start.8 = (f32[8,256,128]{2,1,0:T(8,128)S(1)}, f32[8,256,128]{2,1,0:T(8,128)}, u32[]{:S(2)}) copy-start(f32[8,256,128]{2,1,0:T(8,128)} %copy-done.7) | copy-start | bytes 3145732

commit v2 on v1

--- a/solution.py
+++ b/solution.py
@@ -13,18 +13,25 @@
 F32, BF16 = jnp.float32, jnp.bfloat16
 NT = (((1,), (1,)), ((), ()))
 YS = 4
-ROUNDS = ((0, 1), (2, 3))
-
-
-def pack_kernel(kv_ref, docs_ref, piece_ref, rows_ref):
+
+
+def pack_kernel(kv_ref, docs_ref, piece_ref, rows_ref, docs_vmem, sems):
     tok = kv_ref.shape[1]
-    piece_ref[0:tok] = kv_ref[0]
-    piece_ref[tok : 2 * tok] = kv_ref[1]
-    docs = docs_ref[...].astype(F32)
+    copies = [
+        pltpu.make_async_copy(docs_ref, docs_vmem, sems.at[0]),
+        pltpu.make_async_copy(kv_ref.at[0], piece_ref.at[0:tok], sems.at[1]),
+        pltpu.make_async_copy(kv_ref.at[1], piece_ref.at[tok : 2 * tok], sems.at[2]),
+    ]
+    for copy in copies:
+        copy.start()
+    copies[0].wait()
+    docs = docs_vmem[...].astype(F32) + 1.0
     n = docs.shape[0]
     piece_ref[2 * tok :] = jnp.concatenate([docs, jnp.zeros((16 - n, HD), F32)], 0).astype(BF16)
     for t in range(n):
         rows_ref[t * HD : (t + 1) * HD] = jnp.broadcast_to(docs[t : t + 1], (HD, HD)).T
+    copies[1].wait()
+    copies[2].wait()
 
 
 def key_docs(piece_ref, lead, tok):
@@ -65,7 +72,7 @@
     bias = [jnp.where(key_docs(r, i, tok) == first, 0.0, -FAR) for r, i in pieces]
 
     def score(h, slot):
-        q = q_ref[:, pl.ds(pl.multiple_of(h * HD, HD), HD)]
+        q = q_ref[:, h * HD : (h + 1) * HD]
         mx = None
         for k, (r, i) in enumerate(pieces):
             s = lax.dot_general(q, r[i + (slice(0, tok),)], NT, preferred_element_type=F32) + bias[k]
@@ -90,50 +97,48 @@
         acc = acc_in[h] * alpha + o[:, :HD]
         total = l_in[h] * alpha + o[:, HD:]
         if last:
-            outs[0][:, pl.ds(pl.multiple_of(h * HD, HD), HD)] = (acc / total).astype(BF16)
+            outs[0][:, h * HD : (h + 1) * HD] = (acc / total).astype(BF16)
         else:
             outs[0][h] = m_new
             outs[1][h] = total
             outs[2][h] = acc
 
     score(0, 0)
-
-    def step(h, _):
-        score(jnp.minimum(h + 1, heads - 1), (h + 1) % 2)
+    for h in range(heads):
+        if h + 1 < heads:
+            score(h + 1, (h + 1) % 2)
         finish(h, h % 2)
-        return 0
-
-    lax.fori_loop(0, heads, step, 0)
 
 
 def lay_kernel(count, *refs):
-    levels, out = refs[:-1], refs[-1]
+    levels, outs = refs[: count + 1], refs[count + 1 :]
     y = lax.axis_index("ctx") % YS
-    for slot in range(YS):
+    for by, out in enumerate(outs, 1):
         for k in range(count):
 
-            @pl.when(slot > y)
+            @pl.when(y + by < YS)
             def _():
-                out[slot, k] = levels[k][...]
-
-            @pl.when(slot <= y)
+                out[k] = levels[k][...]
+
+            @pl.when(y + by >= YS)
             def _():
-                out[slot, k] = levels[k + 1][...]
+                out[k] = levels[k + 1][...]
 
 
 VM = pl.BlockSpec(memory_space=pltpu.VMEM)
 
 
-def params():
-    return pltpu.CompilerParams(vmem_limit_bytes=40 * 2**20)
+def params(mib=24):
+    return pltpu.CompilerParams(vmem_limit_bytes=mib * 2**20)
 
 
 def pack(kv, docs):
     tok = kv.shape[1]
     return pl.pallas_call(
         pack_kernel,
-        in_specs=[VM, VM],
+        in_specs=[pl.BlockSpec(memory_space=pl.ANY)] * 2,
         out_specs=[VM, VM],
+        scratch_shapes=[pltpu.VMEM(docs.shape, docs.dtype), pltpu.SemaphoreType.DMA((3,))],
         out_shape=[jax.ShapeDtypeStruct((2 * tok + 16, HD), BF16), jax.ShapeDtypeStruct((tok, HD), F32)],
         compiler_params=params(),
         name="pack",
@@ -181,8 +186,8 @@
     return pl.pallas_call(
         functools.partial(lay_kernel, count),
         in_specs=[VM] * len(levels),
-        out_specs=VM,
-        out_shape=jax.ShapeDtypeStruct((YS, count, *levels[0].shape), BF16),
+        out_specs=[VM] * (YS - 1),
+        out_shape=[jax.ShapeDtypeStruct((count, *levels[0].shape), BF16)] * (YS - 1),
         compiler_params=params(),
         name="lay",
     )(*levels)
@@ -190,18 +195,26 @@
 
 def on_device(queries, keys_values, segments):
     size = lax.axis_size("ctx")
-    up = [(c, (c + YS) % size) for c in range(size)]
-    groups = [list(range(c, c + YS)) for c in range(0, size, YS)]
+
+    def up(x, by):
+        return lax.ppermute(x, "ctx", [(c, c + by * YS) for c in range(size - by * YS)])
+
+    def across(x, by):
+        return lax.ppermute(x, "ctx", [(c, c - c % YS + (c + by) % YS) for c in range(size)])
+
     piece, rows = pack(keys_values, segments.reshape(-1, HD))
-    levels = [piece]
-    for _ in range(ROUNDS[-1][-1] + 1):
-        levels.append(lax.ppermute(levels[-1], "ctx", up))
+    two = up(piece, 2)
+    one = up(piece, 1)
     carry = own(queries, rows, piece)
-    for wanted in ROUNDS:
-        sent = lay(levels[wanted[0] : wanted[-1] + 2])
-        got = lax.all_to_all(sent, "ctx", 0, 0, axis_index_groups=groups)
-        carry = far(queries, rows, [got], carry, wanted is ROUNDS[-1])
-    return carry
+    two, carry = lax.optimization_barrier((two, carry))
+    both = up(jnp.stack([one, two]), 2)
+    near = [across(x, by) for by, x in enumerate(lay([piece, one, two]), 1)]
+    carry = far(queries, rows, [one, two], carry, False)
+    both, carry = lax.optimization_barrier((both, carry))
+    away = [across(x, by) for by, x in enumerate(lay([two, both[0], both[1]]), 1)]
+    carry = far(queries, rows, [both, *near], carry, False)
+    carry = far(queries, rows, [away[0], away[2]], carry, False)
+    return far(queries, rows, [away[1]], carry, True)
 
 
 def solution(mesh):

time: 85.8 us -> 61.5 us (0.72)
  the two profiles are of different devices: /device:TPU:12 before, /device:TPU:92 now
where the time goes in v2:
time: 61.5 us; the launch traced here: 61.1 us
  starting transfers between devices  35.8 us (58%)
  Pallas kernels  15.1 us (25%)
  waiting for transfers between devices  7.32 us (12%)
  local copies, waits for them, and re-layouts  2.64 us (4%)
    ppermute x6, starting transfers between devices, across(): lax.ppermute(x, 'ctx', [(c, c - c % YS + (c + by) % YS) for c in range(si...  19 us
    ppermute x3, starting transfers between devices, up(): lax.ppermute(x, 'ctx', [(c, c + by * YS) for c in range(size - by * YS)])  16.9 us
    pallas_call x4, Pallas kernels, far(): pl.pallas_call(functools.partial(far_kernel, last, len(pieces)), in_specs...  13.6 us
    ppermute x6, waiting for transfers between devices, across(): lax.ppermute(x, 'ctx', [(c, c - c % YS + (c + by) % YS) for c in range(si...  3.83 us
    ppermute x3, waiting for transfers between devices, up(): lax.ppermute(x, 'ctx', [(c, c + by * YS) for c in range(size - by * YS)])  3.49 us
    unnamed x8, local copies, waits for them, and re-layouts  2.63 us
  transfers between devices with their start and end apart: 9, of which 4 were waited for; matrix products, arithmetic and copies ran while one was open for 0% of the time, Pallas kernels for 20%

profile of v2, /device:TPU:92, one launch (start us, length us, event | category | flops | bytes accessed | tf_op | source)
XLA Modules:
  0.0 61.1 jit_solution(9632668240827534476)
XLA Ops:
  0.0 0.7 %copy-done.3 = s32[256]{0:T(256)S(1)} copy-done((s32[256]{0:T(256)S(1)}, s32[256]{0:T(256)}, u32[]{:S(2)}) %copy-start.3) | copy-done | bytes 1048
  0.7 0.9 %copy-done.2 = bf16[2,256,128]{2,1,0:T(8,128)(2,1)S(1)} copy-done((bf16[2,256,128]{2,1,0:T(8,128)(2,1)S(1)}, bf16[2,256,128]{2,1,0:T(8,128)(2,1)}, u32[]{:S(2)}) %copy-start.2) | copy-done | bytes 131096
  1.6 0.3 pack.1
  1.9 6.4 %collective-permute-start = (bf16[528,128]{1,0:T(8,128)(2,1)S(1)}, bf16[528,128]{1,0:T(8,128)(2,1)S(1)}, u32[]{:S(2)}, u32[]{:S(2)}) collective-permute-start(bf16[528,128]{1,0:T(8,128)(2,1)S(1)} %get-tuple-element.34.piece_ref.refs_0_), channel_id=1, source_target_pairs={{0,64},{8,72},{16,80},{24,88},{32,96},{40,104},{48,112},{56,120},{... | collective-permute-start | bytes 405512 | tf_op jit(solution)/shard_map/ppermute | solution.py:200
  8.3 3.8 %collective-permute-start.1 = (bf16[528,128]{1,0:T(8,128)(2,1)S(1)}, bf16[528,128]{1,0:T(8,128)(2,1)S(1)}, u32[]{:S(2)}, u32[]{:S(2)}) collective-permute-start(bf16[528,128]{1,0:T(8,128)(2,1)S(1)} %get-tuple-element.34.piece_ref.refs_0_), channel_id=1, source_target_pairs={{0,32},{8,40},{16,48},{24,56},{32,64},{40,72},{48,80},{56,88},{64,... | collective-permute-start | bytes 405512 | tf_op jit(solution)/shard_map/ppermute | solution.py:200
  12.1 0.0 copy-start
  12.1 1.0 %copy-done = bf16[256,1024]{1,0:T(8,128)(2,1)S(1)} copy-done((bf16[256,1024]{1,0:T(8,128)(2,1)S(1)}, bf16[256,1024]{1,0:T(8,128)(2,1)}, u32[]{:S(2)}) %copy-start) | copy-done | bytes 524312
  13.1 1.0 %own.1 = (f32[8,256,128]{2,1,0:T(8,128)S(1)}, f32[8,256,128]{2,1,0:T(8,128)S(1)}, f32[8,256,128]{2,1,0:T(8,128)S(1)}) custom-call(bf16[256,1024]{1,0:T(8,128)(2,1)S(1)} %copy-done, f32[256,128]{1,0:T(8,128)S(1)} %get-tuple-element.33.rows_ref.refs_1_, bf16[528,128]{1,0:T(8,128)(2,1)S(1)} %get-tuple-element.34.piece_ref.refs_0_), custom_call_target="tpu_custom_call" | custom-call | flops 268435456 | bytes 1048576 | tf_op jit(solution)/shard_map/own/pallas_call | solution.py:158
  14.1 0.0 copy-start.1
  14.1 0.7 %collective-permute-done.refs_3_.refs_0_.refs_2_ = bf16[528,128]{1,0:T(8,128)(2,1)S(1)} collective-permute-done((bf16[528,128]{1,0:T(8,128)(2,1)S(1)}, bf16[528,128]{1,0:T(8,128)(2,1)S(1)}, u32[]{:S(2)}, u32[]{:S(2)}) %collective-permute-start) | collective-permute-done | bytes 135200 | tf_op jit(solution)/shard_map/ppermute | solution.py:200
  14.9 1.9 %collective-permute-done.1.refs_2_.refs_1_ = bf16[528,128]{1,0:T(8,128)(2,1)S(1)} collective-permute-done((bf16[528,128]{1,0:T(8,128)(2,1)S(1)}, bf16[528,128]{1,0:T(8,128)(2,1)S(1)}, u32[]{:S(2)}, u32[]{:S(2)}) %collective-permute-start.1) | collective-permute-done | bytes 135200 | tf_op jit(solution)/shard_map/ppermute | solution.py:200
  16.8 6.6 %collective-permute-start.2 = (bf16[2,528,128]{2,1,0:T(8,128)(2,1)S(1)}, bf16[2,528,128]{2,1,0:T(8,128)(2,1)S(1)}, u32[]{:S(2)}, u32[]{:S(2)}) collective-permute-start(bf16[2,528,128]{2,1,0:T(8,128)(2,1)S(1)} %pad_maximum_fusion), channel_id=1, source_target_pairs={{0,64},{8,72},{16,80},{24,88},{32,96},{40,104},{48,112},{56,120},{... | collective-permute-start | bytes 811016 | tf_op jit(solution)/shard_map/ppermute | solution.py:200
  23.5 0.1 lay.3
  23.6 2.1 %collective-permute-start.6 = (bf16[2,528,128]{2,1,0:T(8,128)(2,1)S(1)}, bf16[2,528,128]{2,1,0:T(8,128)(2,1)S(1)}, u32[]{:S(2)}, u32[]{:S(2)}) collective-permute-start(bf16[2,528,128]{2,1,0:T(8,128)(2,1)S(1)} %get-tuple-element.49), channel_id=1, source_target_pairs={{0,8},{8,16},{16,24},{24,0},{32,40},{40,48},{48,56},{56,32},{64,72... | collective-permute-start | bytes 811016 | tf_op jit(solution)/shard_map/ppermute | solution.py:203
  25.7 4.5 %collective-permute-start.7 = (bf16[2,528,128]{2,1,0:T(8,128)(2,1)S(1)}, bf16[2,528,128]{2,1,0:T(8,128)(2,1)S(1)}, u32[]{:S(2)}, u32[]{:S(2)}) collective-permute-start(bf16[2,528,128]{2,1,0:T(8,128)(2,1)S(1)} %get-tuple-element.50), channel_id=1, source_target_pairs={{0,16},{8,24},{16,0},{24,8},{32,48},{40,56},{48,32},{56,40},{64,80... | collective-permute-start | bytes 811016 | tf_op jit(solution)/shard_map/ppermute | solution.py:203
  30.2 1.9 %collective-permute-start.8 = (bf16[2,528,128]{2,1,0:T(8,128)(2,1)S(1)}, bf16[2,528,128]{2,1,0:T(8,128)(2,1)S(1)}, u32[]{:S(2)}, u32[]{:S(2)}) collective-permute-start(bf16[2,528,128]{2,1,0:T(8,128)(2,1)S(1)} %get-tuple-element.51), channel_id=1, source_target_pairs={{0,24},{8,0},{16,8},{24,16},{32,56},{40,32},{48,40},{56,48},{64,88... | collective-permute-start | bytes 811016 | tf_op jit(solution)/shard_map/ppermute | solution.py:203
  32.1 0.0 copy-done.1
  32.2 2.0 %far.4 = (f32[8,256,128]{2,1,0:T(8,128)S(1)}, f32[8,256,128]{2,1,0:T(8,128)S(1)}, f32[8,256,128]{2,1,0:T(8,128)S(1)}) custom-call(bf16[256,1024]{1,0:T(8,128)(2,1)S(1)} %copy-done.1, f32[256,128]{1,0:T(8,128)S(1)} %get-tuple-element.33.rows_ref.refs_1_, bf16[528,128]{1,0:T(8,128)(2,1)S(1)} %collective-permute-done.1.refs_2_.refs_1_, ...), custom_call_target="tpu_custom_call" | custom-call | flops 536870912 | bytes 1048576 | tf_op jit(solution)/shard_map/far/pallas_call | solution.py:172
  34.1 0.8 %collective-permute-done.2.refs_2_ = bf16[2,528,128]{2,1,0:T(8,128)(2,1)S(1)} collective-permute-done((bf16[2,528,128]{2,1,0:T(8,128)(2,1)S(1)}, bf16[2,528,128]{2,1,0:T(8,128)(2,1)S(1)}, u32[]{:S(2)}, u32[]{:S(2)}) %collective-permute-start.2) | collective-permute-done | bytes 270368 | tf_op jit(solution)/shard_map/ppermute | solution.py:200
  35.0 0.1 lay.2
  35.1 4.3 %collective-permute-start.4 = (bf16[2,528,128]{2,1,0:T(8,128)(2,1)S(1)}, bf16[2,528,128]{2,1,0:T(8,128)(2,1)S(1)}, u32[]{:S(2)}, u32[]{:S(2)}) collective-permute-start(bf16[2,528,128]{2,1,0:T(8,128)(2,1)S(1)} %get-tuple-element.47), channel_id=1, source_target_pairs={{0,8},{8,16},{16,24},{24,0},{32,40},{40,48},{48,56},{56,32},{64,72... | collective-permute-start | bytes 811016 | tf_op jit(solution)/shard_map/ppermute | solution.py:203
  39.4 1.9 %collective-permute-start.5 = (bf16[2,528,128]{2,1,0:T(8,128)(2,1)S(1)}, bf16[2,528,128]{2,1,0:T(8,128)(2,1)S(1)}, u32[]{:S(2)}, u32[]{:S(2)}) collective-permute-start(bf16[2,528,128]{2,1,0:T(8,128)(2,1)S(1)} %get-tuple-element.48), channel_id=1, source_target_pairs={{0,24},{8,0},{16,8},{24,16},{32,56},{40,32},{48,40},{56,48},{64,88... | collective-permute-start | bytes 811016 | tf_op jit(solution)/shard_map/ppermute | solution.py:203
  41.4 0.0 collective-permute-done.6.refs_3_
  41.4 4.2 %collective-permute-start.3 = (bf16[2,528,128]{2,1,0:T(8,128)(2,1)S(1)}, bf16[2,528,128]{2,1,0:T(8,128)(2,1)S(1)}, u32[]{:S(2)}, u32[]{:S(2)}) collective-permute-start(bf16[2,528,128]{2,1,0:T(8,128)(2,1)S(1)} %get-tuple-element.46), channel_id=1, source_target_pairs={{0,16},{8,24},{16,0},{24,8},{32,48},{40,56},{48,32},{56,40},{64,80... | collective-permute-start | bytes 811016 | tf_op jit(solution)/shard_map/ppermute | solution.py:203
  45.6 0.0 collective-permute-done.7.refs_4_
  45.6 0.0 collective-permute-done.8.refs_5_
  45.6 5.8 %far.5 = (f32[8,256,128]{2,1,0:T(8,128)S(1)}, f32[8,256,128]{2,1,0:T(8,128)S(1)}, f32[8,256,128]{2,1,0:T(8,128)S(1)}) custom-call(bf16[256,1024]{1,0:T(8,128)(2,1)S(1)} %copy-done.1, f32[256,128]{1,0:T(8,128)S(1)} %get-tuple-element.33.rows_ref.refs_1_, bf16[2,528,128]{2,1,0:T(8,128)(2,1)S(1)} %collective-permute-done.2.refs_2_, ...), custom_call_target="tpu_custom_call" | custom-call | flops 2147483648 | bytes 1048576 | tf_op jit(solution)/shard_map/far/pallas_call | solution.py:172
  51.4 0.0 collective-permute-done.4.refs_2_
  51.4 3.8 %collective-permute-done.5.refs_3_ = bf16[2,528,128]{2,1,0:T(8,128)(2,1)S(1)} collective-permute-done((bf16[2,528,128]{2,1,0:T(8,128)(2,1)S(1)}, bf16[2,528,128]{2,1,0:T(8,128)(2,1)S(1)}, u32[]{:S(2)}, u32[]{:S(2)}) %collective-permute-start.5) | collective-permute-done | bytes 270368 | tf_op jit(solution)/shard_map/ppermute | solution.py:203
  55.2 3.0 %far.6 = (f32[8,256,128]{2,1,0:T(8,128)S(1)}, f32[8,256,128]{2,1,0:T(8,128)S(1)}, f32[8,256,128]{2,1,0:T(8,128)S(1)}) custom-call(bf16[256,1024]{1,0:T(8,128)(2,1)S(1)} %copy-done.1, f32[256,128]{1,0:T(8,128)S(1)} %get-tuple-element.33.rows_ref.refs_1_, bf16[2,528,128]{2,1,0:T(8,128)(2,1)S(1)} %collective-permute-done.4.refs_2_, ...), custom_call_target="tpu_custom_call" | custom-call | flops 1073741824 | bytes 1048576 | tf_op jit(solution)/shard_map/far/pallas_call | solution.py:172
  58.2 0.0 collective-permute-done.3.refs_2_
  58.2 2.9 %far.7 = bf16[256,1024]{1,0:T(8,128)(2,1)} custom-call(bf16[256,1024]{1,0:T(8,128)(2,1)S(1)} %copy-done.1, f32[256,128]{1,0:T(8,128)S(1)} %get-tuple-element.33.rows_ref.refs_1_, bf16[2,528,128]{2,1,0:T(8,128)(2,1)S(1)} %collective-permute-done.3.refs_2_, f32[8,256,128]{2,1,0:T(8,128)S(1)} %get-tuple-element.58.refs_3_, ...), custom_call_target="tpu_custom_call" | custom-call | flops 536870912 | bytes 1048576 | tf_op jit(solution)/shard_map/far/pallas_call | solution.py:172
  (4 shorter events, 0.0 us)
Async XLA Ops:
  0.0 0.7 %copy-start.3 = (s32[256]{0:T(256)S(1)}, s32[256]{0:T(256)}, u32[]{:S(2)}) copy-start(s32[256]{0:T(256)} %param.5) | copy-start | bytes 3076
  0.7 0.9 %copy-start.2 = (bf16[2,256,128]{2,1,0:T(8,128)(2,1)S(1)}, bf16[2,256,128]{2,1,0:T(8,128)(2,1)}, u32[]{:S(2)}) copy-start(bf16[2,256,128]{2,1,0:T(8,128)(2,1)} %kv_ref.1) | copy-start | bytes 393220
  1.9 13.0 %collective-permute-start = (bf16[528,128]{1,0:T(8,128)(2,1)S(1)}, bf16[528,128]{1,0:T(8,128)(2,1)S(1)}, u32[]{:S(2)}, u32[]{:S(2)}) collective-permute-start(bf16[528,128]{1,0:T(8,128)(2,1)S(1)} %get-tuple-element.34.piece_ref.refs_0_), channel_id=1, source_target_pairs={{0,64},{8,72},{16,80},{24,88},{32,96},{40,104},{48,112},{56,120},{... | collective-permute-start | bytes 405512 | tf_op jit(solution)/shard_map/ppermute | solution.py:200
  8.3 8.5 %collective-permute-start.1 = (bf16[528,128]{1,0:T(8,128)(2,1)S(1)}, bf16[528,128]{1,0:T(8,128)(2,1)S(1)}, u32[]{:S(2)}, u32[]{:S(2)}) collective-permute-start(bf16[528,128]{1,0:T(8,128)(2,1)S(1)} %get-tuple-element.34.piece_ref.refs_0_), channel_id=1, source_target_pairs={{0,32},{8,40},{16,48},{24,56},{32,64},{40,72},{48,80},{56,88},{64,... | collective-permute-start | bytes 405512 | tf_op jit(solution)/shard_map/ppermute | solution.py:200
  12.1 1.0 %copy-start = (bf16[256,1024]{1,0:T(8,128)(2,1)S(1)}, bf16[256,1024]{1,0:T(8,128)(2,1)}, u32[]{:S(2)}) copy-start(bf16[256,1024]{1,0:T(8,128)(2,1)} %refs_0_.7) | copy-start | bytes 1572868
  14.1 18.0 %copy-start.1 = (bf16[256,1024]{1,0:T(8,128)(2,1)S(1)}, bf16[256,1024]{1,0:T(8,128)(2,1)}, u32[]{:S(2)}) copy-start(bf16[256,1024]{1,0:T(8,128)(2,1)} %refs_0_.7) | copy-start | bytes 1572868
  16.8 18.2 %collective-permute-start.2 = (bf16[2,528,128]{2,1,0:T(8,128)(2,1)S(1)}, bf16[2,528,128]{2,1,0:T(8,128)(2,1)S(1)}, u32[]{:S(2)}, u32[]{:S(2)}) collective-permute-start(bf16[2,528,128]{2,1,0:T(8,128)(2,1)S(1)} %pad_maximum_fusion), channel_id=1, source_target_pairs={{0,64},{8,72},{16,80},{24,88},{32,96},{40,104},{48,112},{56,120},{... | collective-permute-start | bytes 811016 | tf_op jit(solution)/shard_map/ppermute | solution.py:200
  23.6 17.8 %collective-permute-start.6 = (bf16[2,528,128]{2,1,0:T(8,128)(2,1)S(1)}, bf16[2,528,128]{2,1,0:T(8,128)(2,1)S(1)}, u32[]{:S(2)}, u32[]{:S(2)}) collective-permute-start(bf16[2,528,128]{2,1,0:T(8,128)(2,1)S(1)} %get-tuple-element.49), channel_id=1, source_target_pairs={{0,8},{8,16},{16,24},{24,0},{32,40},{40,48},{48,56},{56,32},{64,72... | collective-permute-start | bytes 811016 | tf_op jit(solution)/shard_map/ppermute | solution.py:203
  25.7 19.9 %collective-permute-start.7 = (bf16[2,528,128]{2,1,0:T(8,128)(2,1)S(1)}, bf16[2,528,128]{2,1,0:T(8,128)(2,1)S(1)}, u32[]{:S(2)}, u32[]{:S(2)}) collective-permute-start(bf16[2,528,128]{2,1,0:T(8,128)(2,1)S(1)} %get-tuple-element.50), channel_id=1, source_target_pairs={{0,16},{8,24},{16,0},{24,8},{32,48},{40,56},{48,32},{56,40},{64,80... | collective-permute-start | bytes 811016 | tf_op jit(solution)/shard_map/ppermute | solution.py:203
  30.2 15.4 %collective-permute-start.8 = (bf16[2,528,128]{2,1,0:T(8,128)(2,1)S(1)}, bf16[2,528,128]{2,1,0:T(8,128)(2,1)S(1)}, u32[]{:S(2)}, u32[]{:S(2)}) collective-permute-start(bf16[2,528,128]{2,1,0:T(8,128)(2,1)S(1)} %get-tuple-element.51), channel_id=1, source_target_pairs={{0,24},{8,0},{16,8},{24,16},{32,56},{40,32},{48,40},{56,48},{64,88... | collective-permute-start | bytes 811016 | tf_op jit(solution)/shard_map/ppermute | solution.py:203
  35.1 16.3 %collective-permute-start.4 = (bf16[2,528,128]{2,1,0:T(8,128)(2,1)S(1)}, bf16[2,528,128]{2,1,0:T(8,128)(2,1)S(1)}, u32[]{:S(2)}, u32[]{:S(2)}) collective-permute-start(bf16[2,528,128]{2,1,0:T(8,128)(2,1)S(1)} %get-tuple-element.47), channel_id=1, source_target_pairs={{0,8},{8,16},{16,24},{24,0},{32,40},{40,48},{48,56},{56,32},{64,72... | collective-permute-start | bytes 811016 | tf_op jit(solution)/shard_map/ppermute | solution.py:203
  39.4 15.8 %collective-permute-start.5 = (bf16[2,528,128]{2,1,0:T(8,128)(2,1)S(1)}, bf16[2,528,128]{2,1,0:T(8,128)(2,1)S(1)}, u32[]{:S(2)}, u32[]{:S(2)}) collective-permute-start(bf16[2,528,128]{2,1,0:T(8,128)(2,1)S(1)} %get-tuple-element.48), channel_id=1, source_target_pairs={{0,24},{8,0},{16,8},{24,16},{32,56},{40,32},{48,40},{56,48},{64,88... | collective-permute-start | bytes 811016 | tf_op jit(solution)/shard_map/ppermute | solution.py:203
  41.4 16.9 %collective-permute-start.3 = (bf16[2,528,128]{2,1,0:T(8,128)(2,1)S(1)}, bf16[2,528,128]{2,1,0:T(8,128)(2,1)S(1)}, u32[]{:S(2)}, u32[]{:S(2)}) collective-permute-start(bf16[2,528,128]{2,1,0:T(8,128)(2,1)S(1)} %get-tuple-element.46), channel_id=1, source_target_pairs={{0,16},{8,24},{16,0},{24,8},{32,48},{40,56},{48,32},{56,40},{64,80... | collective-permute-start | bytes 811016 | tf_op jit(solution)/shard_map/ppermute | solution.py:203

commit v3 on v2

--- a/solution.py
+++ b/solution.py
@@ -1,5 +1,4 @@
 import functools
-import itertools
 import jax
 import jax.numpy as jnp
 from jax import lax
@@ -58,56 +57,95 @@
         l_ref[h] = o[:, HD:]
 
 
-def far_kernel(last, n_refs, *refs):
+def far_kernel(last, tiers, n_refs, *refs):
     q_ref, rows_ref = refs[:2]
     piece_refs = refs[2 : 2 + n_refs]
-    m_in, l_in, acc_in = refs[2 + n_refs : 5 + n_refs]
-    outs = refs[5 + n_refs : -2]
-    s_ref, mx_ref = refs[-2:]
+    carry_in = refs[2 + n_refs : 5 + n_refs]
+    m_in, l_in, acc_in = carry_in
+    if last:
+        out_hbm, s_ref, mx_ref, result, sems = refs[5 + n_refs :]
+    else:
+        *outs, s_ref, mx_ref = refs[5 + n_refs :]
     tok = q_ref.shape[0]
     heads = q_ref.shape[1] // HD
-    pieces = [(r, i) for r in piece_refs for i in itertools.product(*[range(s) for s in r.shape[:-2]])]
     first = rows_ref[0:1, 0:1]
-    row_off = jnp.where(rows_ref[...] == first, 0.0, FAR)
-    bias = [jnp.where(key_docs(r, i, tok) == first, 0.0, -FAR) for r, i in pieces]
-
-    def score(h, slot):
-        q = q_ref[:, h * HD : (h + 1) * HD]
-        mx = None
-        for k, (r, i) in enumerate(pieces):
-            s = lax.dot_general(q, r[i + (slice(0, tok),)], NT, preferred_element_type=F32) + bias[k]
-            s_ref[slot, :, k * tok : (k + 1) * tok] = s
-            for t in range(tok // HD):
-                part = s[:, t * HD : (t + 1) * HD]
-                mx = part if mx is None else jnp.maximum(mx, part)
-        mx_ref[slot] = mx
-
-    def finish(h, slot):
-        m_old = m_in[h]
-        m_new = jnp.maximum(m_old, jnp.max(mx_ref[slot], 1, keepdims=True) - row_off)
-        alpha = jnp.exp2((m_old - m_new) * FACTOR)
-        shift = jnp.concatenate([m_new + row_off] * (tok // HD), 1) * FACTOR
-        o = None
-        for k, (r, i) in enumerate(pieces):
-            s = s_ref[slot, :, k * tok : (k + 1) * tok]
-            p = jnp.exp2(s * FACTOR - shift).astype(BF16)
-            v = jnp.concatenate([r[i + (slice(tok, 2 * tok),)], jnp.ones((tok, HD), BF16)], 1)
-            d = jnp.dot(p, v, preferred_element_type=F32)
-            o = d if o is None else o + d
-        acc = acc_in[h] * alpha + o[:, :HD]
-        total = l_in[h] * alpha + o[:, HD:]
-        if last:
-            outs[0][:, h * HD : (h + 1) * HD] = (acc / total).astype(BF16)
-        else:
-            outs[0][h] = m_new
-            outs[1][h] = total
-            outs[2][h] = acc
-
-    score(0, 0)
-    for h in range(heads):
-        if h + 1 < heads:
-            score(h + 1, (h + 1) % 2)
-        finish(h, h % 2)
+
+    def leave(h):
+        columns = slice(h * HD, (h + 1) * HD)
+        return pltpu.make_async_copy(result.at[:, columns], out_hbm.at[:, columns], sems.at[h])
+
+    def attend(pieces, bias):
+        row_off = jnp.where(rows_ref[...] == first, 0.0, FAR)
+
+        def score(h, slot):
+            q = q_ref[:, h * HD : (h + 1) * HD]
+            mx = None
+            for k, (r, i) in enumerate(pieces):
+                s = lax.dot_general(q, r[i + (slice(0, tok),)], NT, preferred_element_type=F32) + bias[k]
+                s_ref[slot, :, k * tok : (k + 1) * tok] = s
+                for t in range(tok // HD):
+                    part = s[:, t * HD : (t + 1) * HD]
+                    mx = part if mx is None else jnp.maximum(mx, part)
+            mx_ref[slot] = mx
+
+        def finish(h, slot):
+            m_old = m_in[h]
+            m_new = jnp.maximum(m_old, jnp.max(mx_ref[slot], 1, keepdims=True) - row_off)
+            alpha = jnp.exp2((m_old - m_new) * FACTOR)
+            shift = jnp.concatenate([m_new + row_off] * (tok // HD), 1) * FACTOR
+            o = None
+            for k, (r, i) in enumerate(pieces):
+                s = s_ref[slot, :, k * tok : (k + 1) * tok]
+                p = jnp.exp2(s * FACTOR - shift).astype(BF16)
+                v = jnp.concatenate([r[i + (slice(tok, 2 * tok),)], jnp.ones((tok, HD), BF16)], 1)
+                d = jnp.dot(p, v, preferred_element_type=F32)
+                o = d if o is None else o + d
+            acc = acc_in[h] * alpha + o[:, :HD]
+            total = l_in[h] * alpha + o[:, HD:]
+            if last:
+                result[:, h * HD : (h + 1) * HD] = (acc / total).astype(BF16)
+                leave(h).start()
+            else:
+                outs[0][h] = m_new
+                outs[1][h] = total
+                outs[2][h] = acc
+
+        score(0, 0)
+        for h in range(heads):
+            if h + 1 < heads:
+                score(h + 1, (h + 1) % 2)
+            finish(h, h % 2)
+
+    pieces, bias, seen = [], [], []
+    for tier in tiers:
+        new = [(piece_refs[n], i) for n, i in tier]
+        pieces.append((pieces[-1] if pieces else []) + new)
+        new_bias = [jnp.where(key_docs(r, i, tok) == first, 0.0, -FAR) for r, i in new]
+        bias.append((bias[-1] if bias else []) + new_bias)
+        seen.append(jnp.max(functools.reduce(jnp.maximum, new_bias)) == 0.0)
+
+    farther = jnp.bool_(False)
+    for t in reversed(range(len(tiers))):
+
+        @pl.when(seen[t] & jnp.logical_not(farther))
+        def _():
+            attend(pieces[t], bias[t])
+
+        farther = farther | seen[t]
+
+    @pl.when(jnp.logical_not(farther))
+    def _():
+        for h in range(heads):
+            if last:
+                result[:, h * HD : (h + 1) * HD] = (acc_in[h] / l_in[h]).astype(BF16)
+                leave(h).start()
+            else:
+                for ref, out in zip(carry_in, outs):
+                    out[h] = ref[h]
+
+    if last:
+        for h in range(heads):
+            leave(h).wait()
 
 
 def lay_kernel(count, *refs):
@@ -126,6 +164,7 @@
 
 
 VM = pl.BlockSpec(memory_space=pltpu.VMEM)
+HBM = pl.BlockSpec(memory_space=pltpu.HBM)
 
 
 def params(mib=24):
@@ -166,15 +205,16 @@
     )(q, rows, piece)
 
 
-def far(q, rows, pieces, carry, last):
+def far(q, rows, pieces, tiers, carry, last):
     tok = q.shape[0]
-    n = sum(p.size // (p.shape[-1] * p.shape[-2]) for p in pieces)
-    return pl.pallas_call(
-        functools.partial(far_kernel, last, len(pieces)),
+    n = sum(map(len, tiers))
+    return pl.pallas_call(
+        functools.partial(far_kernel, last, tiers, len(pieces)),
         in_specs=[VM] * (5 + len(pieces)),
-        out_specs=VM if last else [VM] * 3,
+        out_specs=HBM if last else [VM] * 3,
         out_shape=jax.ShapeDtypeStruct(q.shape, BF16) if last else carry_shapes(q),
-        scratch_shapes=[pltpu.VMEM((2, tok, n * tok), F32), pltpu.VMEM((2, tok, HD), F32)],
+        scratch_shapes=[pltpu.VMEM((2, tok, n * tok), F32), pltpu.VMEM((2, tok, HD), F32)]
+        + [pltpu.VMEM(q.shape, BF16), pltpu.SemaphoreType.DMA((q.shape[1] // HD,))] * last,
         compiler_params=params(),
         cost_estimate=cost(q.size // HD, n * tok),
         name="far",
@@ -209,12 +249,20 @@
     two, carry = lax.optimization_barrier((two, carry))
     both = up(jnp.stack([one, two]), 2)
     near = [across(x, by) for by, x in enumerate(lay([piece, one, two]), 1)]
-    carry = far(queries, rows, [one, two], carry, False)
+    carry = far(queries, rows, [one, two], [[(0, ()), (1, ())]], carry, False)
     both, carry = lax.optimization_barrier((both, carry))
     away = [across(x, by) for by, x in enumerate(lay([two, both[0], both[1]]), 1)]
-    carry = far(queries, rows, [both, *near], carry, False)
-    carry = far(queries, rows, [away[0], away[2]], carry, False)
-    return far(queries, rows, [away[1]], carry, True)
+    carry = far(
+        queries,
+        rows,
+        [*near, both],
+        [[(0, (0,)), (1, (0,)), (2, (0,))], [(0, (1,)), (1, (1,)), (2, (1,)), (3, (0,)), (3, (1,))]],
+        carry,
+        False,
+    )
+    carry = far(queries, rows, [away[1]], [[(0, (0,)), (0, (1,))]], carry, False)
+    ends = [[(0, (0,)), (1, (0,)), (0, (1,)), (1, (1,))]]
+    return far(queries, rows, [away[0], away[2]], ends, carry, True)
 
 
 def solution(mesh):

time: 61.5 us -> 59.6 us (0.969)
  the two profiles are of different devices: /device:TPU:92 before, /device:TPU:204 now
where the time goes in v3:
time: 59.6 us; the launch traced here: 59.3 us
  starting transfers between devices  35.3 us (59%)
  Pallas kernels  15.3 us (26%)
  waiting for transfers between devices  5.67 us (10%)
  local copies, waits for them, and re-layouts  2.65 us (4%)
    ppermute x6, starting transfers between devices, across(): lax.ppermute(x, 'ctx', [(c, c - c % YS + (c + by) % YS) for c in range(si...  19.2 us
    ppermute x3, starting transfers between devices, up(): lax.ppermute(x, 'ctx', [(c, c + by * YS) for c in range(size - by * YS)])  16.1 us
    pallas_call x4, Pallas kernels, far(): pl.pallas_call(functools.partial(far_kernel, last, tiers, len(pieces)), i...  13.8 us
    ppermute x3, waiting for transfers between devices, up(): lax.ppermute(x, 'ctx', [(c, c + by * YS) for c in range(size - by * YS)])  2.95 us
    ppermute x6, waiting for transfers between devices, across(): lax.ppermute(x, 'ctx', [(c, c - c % YS + (c + by) % YS) for c in range(si...  2.72 us
    unnamed x8, local copies, waits for them, and re-layouts  2.63 us
  transfers between devices with their start and end apart: 9, of which 5 were waited for; matrix products, arithmetic and copies ran while one was open for 0% of the time, Pallas kernels for 19%

profile of v3, /device:TPU:204, one launch (start us, length us, event | category | flops | bytes accessed | tf_op | source)
XLA Modules:
  0.0 59.3 jit_solution(8956151909754160345)
XLA Ops:
  0.0 0.7 %copy-done.3 = s32[256]{0:T(256)S(1)} copy-done((s32[256]{0:T(256)S(1)}, s32[256]{0:T(256)}, u32[]{:S(2)}) %copy-start.3) | copy-done | bytes 1048
  0.7 0.9 %copy-done.2 = bf16[2,256,128]{2,1,0:T(8,128)(2,1)S(1)} copy-done((bf16[2,256,128]{2,1,0:T(8,128)(2,1)S(1)}, bf16[2,256,128]{2,1,0:T(8,128)(2,1)}, u32[]{:S(2)}) %copy-start.2) | copy-done | bytes 131096
  1.6 0.3 pack.1
  1.9 6.4 %collective-permute-start = (bf16[528,128]{1,0:T(8,128)(2,1)S(1)}, bf16[528,128]{1,0:T(8,128)(2,1)S(1)}, u32[]{:S(2)}, u32[]{:S(2)}) collective-permute-start(bf16[528,128]{1,0:T(8,128)(2,1)S(1)} %get-tuple-element.34.piece_ref.refs_0_), channel_id=1, source_target_pairs={{0,64},{8,72},{16,80},{24,88},{32,96},{40,104},{48,112},{56,120},{... | collective-permute-start | bytes 405512 | tf_op jit(solution)/shard_map/ppermute | solution.py:240
  8.3 2.9 %collective-permute-start.1 = (bf16[528,128]{1,0:T(8,128)(2,1)S(1)}, bf16[528,128]{1,0:T(8,128)(2,1)S(1)}, u32[]{:S(2)}, u32[]{:S(2)}) collective-permute-start(bf16[528,128]{1,0:T(8,128)(2,1)S(1)} %get-tuple-element.34.piece_ref.refs_0_), channel_id=1, source_target_pairs={{0,32},{8,40},{16,48},{24,56},{32,64},{40,72},{48,80},{56,88},{64,... | collective-permute-start | bytes 405512 | tf_op jit(solution)/shard_map/ppermute | solution.py:240
  11.2 0.0 copy-start
  11.2 1.0 %copy-done = bf16[256,1024]{1,0:T(8,128)(2,1)S(1)} copy-done((bf16[256,1024]{1,0:T(8,128)(2,1)S(1)}, bf16[256,1024]{1,0:T(8,128)(2,1)}, u32[]{:S(2)}) %copy-start) | copy-done | bytes 524312
  12.2 1.0 %own.1 = (f32[8,256,128]{2,1,0:T(8,128)S(1)}, f32[8,256,128]{2,1,0:T(8,128)S(1)}, f32[8,256,128]{2,1,0:T(8,128)S(1)}) custom-call(bf16[256,1024]{1,0:T(8,128)(2,1)S(1)} %copy-done, f32[256,128]{1,0:T(8,128)S(1)} %get-tuple-element.33.rows_ref.refs_1_, bf16[528,128]{1,0:T(8,128)(2,1)S(1)} %get-tuple-element.34.piece_ref.refs_0_), custom_call_target="tpu_custom_call" | custom-call | flops 268435456 | bytes 1048576 | tf_op jit(solution)/shard_map/own/pallas_call | solution.py:197
  13.2 0.0 copy-start.1
  13.2 0.8 %collective-permute-done.refs_3_.refs_0_.refs_2_ = bf16[528,128]{1,0:T(8,128)(2,1)S(1)} collective-permute-done((bf16[528,128]{1,0:T(8,128)(2,1)S(1)}, bf16[528,128]{1,0:T(8,128)(2,1)S(1)}, u32[]{:S(2)}, u32[]{:S(2)}) %collective-permute-start) | collective-permute-done | bytes 135200 | tf_op jit(solution)/shard_map/ppermute | solution.py:240
  14.0 2.2 %collective-permute-done.1.refs_2_.refs_1_ = bf16[528,128]{1,0:T(8,128)(2,1)S(1)} collective-permute-done((bf16[528,128]{1,0:T(8,128)(2,1)S(1)}, bf16[528,128]{1,0:T(8,128)(2,1)S(1)}, u32[]{:S(2)}, u32[]{:S(2)}) %collective-permute-start.1) | collective-permute-done | bytes 135200 | tf_op jit(solution)/shard_map/ppermute | solution.py:240
  16.2 6.8 %collective-permute-start.2 = (bf16[2,528,128]{2,1,0:T(8,128)(2,1)S(1)}, bf16[2,528,128]{2,1,0:T(8,128)(2,1)S(1)}, u32[]{:S(2)}, u32[]{:S(2)}) collective-permute-start(bf16[2,528,128]{2,1,0:T(8,128)(2,1)S(1)} %pad_maximum_fusion), channel_id=1, source_target_pairs={{0,64},{8,72},{16,80},{24,88},{32,96},{40,104},{48,112},{56,120},{... | collective-permute-start | bytes 811016 | tf_op jit(solution)/shard_map/ppermute | solution.py:240
  23.0 0.1 lay.3
  23.1 3.5 %collective-permute-start.6 = (bf16[2,528,128]{2,1,0:T(8,128)(2,1)S(1)}, bf16[2,528,128]{2,1,0:T(8,128)(2,1)S(1)}, u32[]{:S(2)}, u32[]{:S(2)}) collective-permute-start(bf16[2,528,128]{2,1,0:T(8,128)(2,1)S(1)} %get-tuple-element.49), channel_id=1, source_target_pairs={{0,8},{8,16},{16,24},{24,0},{32,40},{40,48},{48,56},{56,32},{64,72... | collective-permute-start | bytes 811016 | tf_op jit(solution)/shard_map/ppermute | solution.py:243
  26.6 2.8 %collective-permute-start.7 = (bf16[2,528,128]{2,1,0:T(8,128)(2,1)S(1)}, bf16[2,528,128]{2,1,0:T(8,128)(2,1)S(1)}, u32[]{:S(2)}, u32[]{:S(2)}) collective-permute-start(bf16[2,528,128]{2,1,0:T(8,128)(2,1)S(1)} %get-tuple-element.50), channel_id=1, source_target_pairs={{0,16},{8,24},{16,0},{24,8},{32,48},{40,56},{48,32},{56,40},{64,80... | collective-permute-start | bytes 811016 | tf_op jit(solution)/shard_map/ppermute | solution.py:243
  29.4 4.3 %collective-permute-start.8 = (bf16[2,528,128]{2,1,0:T(8,128)(2,1)S(1)}, bf16[2,528,128]{2,1,0:T(8,128)(2,1)S(1)}, u32[]{:S(2)}, u32[]{:S(2)}) collective-permute-start(bf16[2,528,128]{2,1,0:T(8,128)(2,1)S(1)} %get-tuple-element.51), channel_id=1, source_target_pairs={{0,24},{8,0},{16,8},{24,16},{32,56},{40,32},{48,40},{56,48},{64,88... | collective-permute-start | bytes 811016 | tf_op jit(solution)/shard_map/ppermute | solution.py:243
  33.8 0.0 copy-done.1
  33.8 2.1 %far.4 = (f32[8,256,128]{2,1,0:T(8,128)S(1)}, f32[8,256,128]{2,1,0:T(8,128)S(1)}, f32[8,256,128]{2,1,0:T(8,128)S(1)}) custom-call(bf16[256,1024]{1,0:T(8,128)(2,1)S(1)} %copy-done.1, f32[256,128]{1,0:T(8,128)S(1)} %get-tuple-element.33.rows_ref.refs_1_, bf16[528,128]{1,0:T(8,128)(2,1)S(1)} %collective-permute-done.1.refs_2_.refs_1_, ...), custom_call_target="tpu_custom_call" | custom-call | flops 536870912 | bytes 1048576 | tf_op jit(solution)/shard_map/far/pallas_call | solution.py:211
  35.9 0.0 collective-permute-done.2.refs_5_
  36.0 0.1 lay.2
  36.1 2.5 %collective-permute-start.5 = (bf16[2,528,128]{2,1,0:T(8,128)(2,1)S(1)}, bf16[2,528,128]{2,1,0:T(8,128)(2,1)S(1)}, u32[]{:S(2)}, u32[]{:S(2)}) collective-permute-start(bf16[2,528,128]{2,1,0:T(8,128)(2,1)S(1)} %get-tuple-element.48), channel_id=1, source_target_pairs={{0,16},{8,24},{16,0},{24,8},{32,48},{40,56},{48,32},{56,40},{64,80... | collective-permute-start | bytes 811016 | tf_op jit(solution)/shard_map/ppermute | solution.py:243
  38.6 4.1 %collective-permute-start.3 = (bf16[2,528,128]{2,1,0:T(8,128)(2,1)S(1)}, bf16[2,528,128]{2,1,0:T(8,128)(2,1)S(1)}, u32[]{:S(2)}, u32[]{:S(2)}) collective-permute-start(bf16[2,528,128]{2,1,0:T(8,128)(2,1)S(1)} %get-tuple-element.46), channel_id=1, source_target_pairs={{0,8},{8,16},{16,24},{24,0},{32,40},{40,48},{48,56},{56,32},{64,72... | collective-permute-start | bytes 811016 | tf_op jit(solution)/shard_map/ppermute | solution.py:243
  42.7 0.0 collective-permute-done.6.refs_2_
  42.7 1.9 %collective-permute-start.4 = (bf16[2,528,128]{2,1,0:T(8,128)(2,1)S(1)}, bf16[2,528,128]{2,1,0:T(8,128)(2,1)S(1)}, u32[]{:S(2)}, u32[]{:S(2)}) collective-permute-start(bf16[2,528,128]{2,1,0:T(8,128)(2,1)S(1)} %get-tuple-element.47), channel_id=1, source_target_pairs={{0,24},{8,0},{16,8},{24,16},{32,56},{40,32},{48,40},{56,48},{64,88... | collective-permute-start | bytes 811016 | tf_op jit(solution)/shard_map/ppermute | solution.py:243
  44.7 0.0 collective-permute-done.7.refs_3_
  44.7 0.5 collective-permute-done.8.refs_4_
  45.1 5.5 %far.5 = (f32[8,256,128]{2,1,0:T(8,128)S(1)}, f32[8,256,128]{2,1,0:T(8,128)S(1)}, f32[8,256,128]{2,1,0:T(8,128)S(1)}) custom-call(bf16[256,1024]{1,0:T(8,128)(2,1)S(1)} %copy-done.1, f32[256,128]{1,0:T(8,128)S(1)} %get-tuple-element.33.rows_ref.refs_1_, bf16[2,528,128]{2,1,0:T(8,128)(2,1)S(1)} %collective-permute-done.6.refs_2_, ...), custom_call_target="tpu_custom_call" | custom-call | flops 2147483648 | bytes 1048576 | tf_op jit(solution)/shard_map/far/pallas_call | solution.py:211
  50.6 0.5 collective-permute-done.5.refs_2_
  51.1 2.2 %far.6 = (f32[8,256,128]{2,1,0:T(8,128)S(1)}, f32[8,256,128]{2,1,0:T(8,128)S(1)}, f32[8,256,128]{2,1,0:T(8,128)S(1)}) custom-call(bf16[256,1024]{1,0:T(8,128)(2,1)S(1)} %copy-done.1, f32[256,128]{1,0:T(8,128)S(1)} %get-tuple-element.33.rows_ref.refs_1_, bf16[2,528,128]{2,1,0:T(8,128)(2,1)S(1)} %collective-permute-done.5.refs_2_, ...), custom_call_target="tpu_custom_call" | custom-call | flops 536870912 | bytes 1048576 | tf_op jit(solution)/shard_map/far/pallas_call | solution.py:211
  53.3 0.0 collective-permute-done.3.refs_2_
  53.3 1.8 %collective-permute-done.4.refs_3_ = bf16[2,528,128]{2,1,0:T(8,128)(2,1)S(1)} collective-permute-done((bf16[2,528,128]{2,1,0:T(8,128)(2,1)S(1)}, bf16[2,528,128]{2,1,0:T(8,128)(2,1)S(1)}, u32[]{:S(2)}, u32[]{:S(2)}) %collective-permute-start.4) | collective-permute-done | bytes 270368 | tf_op jit(solution)/shard_map/ppermute | solution.py:243
  55.1 4.0 %far.7 = bf16[256,1024]{1,0:T(8,128)(2,1)} custom-call(bf16[256,1024]{1,0:T(8,128)(2,1)S(1)} %copy-done.1, f32[256,128]{1,0:T(8,128)S(1)} %get-tuple-element.33.rows_ref.refs_1_, bf16[2,528,128]{2,1,0:T(8,128)(2,1)S(1)} %collective-permute-done.3.refs_2_, bf16[2,528,128]{2,1,0:T(8,128)(2,1)S(1)} %collective-permute-done.4.refs_3_, ...), custom_call_target="tpu_custom_call" | custom-call | flops 1073741824 | bytes 1048576 | tf_op jit(solution)/shard_map/far/pallas_call | solution.py:211
  (4 shorter events, 0.1 us)
Async XLA Ops:
  0.0 0.7 %copy-start.3 = (s32[256]{0:T(256)S(1)}, s32[256]{0:T(256)}, u32[]{:S(2)}) copy-start(s32[256]{0:T(256)} %param.5) | copy-start | bytes 3076
  0.7 0.9 %copy-start.2 = (bf16[2,256,128]{2,1,0:T(8,128)(2,1)S(1)}, bf16[2,256,128]{2,1,0:T(8,128)(2,1)}, u32[]{:S(2)}) copy-start(bf16[2,256,128]{2,1,0:T(8,128)(2,1)} %kv_ref.1) | copy-start | bytes 393220
  1.9 12.1 %collective-permute-start = (bf16[528,128]{1,0:T(8,128)(2,1)S(1)}, bf16[528,128]{1,0:T(8,128)(2,1)S(1)}, u32[]{:S(2)}, u32[]{:S(2)}) collective-permute-start(bf16[528,128]{1,0:T(8,128)(2,1)S(1)} %get-tuple-element.34.piece_ref.refs_0_), channel_id=1, source_target_pairs={{0,64},{8,72},{16,80},{24,88},{32,96},{40,104},{48,112},{56,120},{... | collective-permute-start | bytes 405512 | tf_op jit(solution)/shard_map/ppermute | solution.py:240
  8.3 7.9 %collective-permute-start.1 = (bf16[528,128]{1,0:T(8,128)(2,1)S(1)}, bf16[528,128]{1,0:T(8,128)(2,1)S(1)}, u32[]{:S(2)}, u32[]{:S(2)}) collective-permute-start(bf16[528,128]{1,0:T(8,128)(2,1)S(1)} %get-tuple-element.34.piece_ref.refs_0_), channel_id=1, source_target_pairs={{0,32},{8,40},{16,48},{24,56},{32,64},{40,72},{48,80},{56,88},{64,... | collective-permute-start | bytes 405512 | tf_op jit(solution)/shard_map/ppermute | solution.py:240
  11.2 1.0 %copy-start = (bf16[256,1024]{1,0:T(8,128)(2,1)S(1)}, bf16[256,1024]{1,0:T(8,128)(2,1)}, u32[]{:S(2)}) copy-start(bf16[256,1024]{1,0:T(8,128)(2,1)} %refs_0_.7) | copy-start | bytes 1572868
  13.2 20.5 %copy-start.1 = (bf16[256,1024]{1,0:T(8,128)(2,1)S(1)}, bf16[256,1024]{1,0:T(8,128)(2,1)}, u32[]{:S(2)}) copy-start(bf16[256,1024]{1,0:T(8,128)(2,1)} %refs_0_.7) | copy-start | bytes 1572868
  16.2 19.7 %collective-permute-start.2 = (bf16[2,528,128]{2,1,0:T(8,128)(2,1)S(1)}, bf16[2,528,128]{2,1,0:T(8,128)(2,1)S(1)}, u32[]{:S(2)}, u32[]{:S(2)}) collective-permute-start(bf16[2,528,128]{2,1,0:T(8,128)(2,1)S(1)} %pad_maximum_fusion), channel_id=1, source_target_pairs={{0,64},{8,72},{16,80},{24,88},{32,96},{40,104},{48,112},{56,120},{... | collective-permute-start | bytes 811016 | tf_op jit(solution)/shard_map/ppermute | solution.py:240
  23.1 19.6 %collective-permute-start.6 = (bf16[2,528,128]{2,1,0:T(8,128)(2,1)S(1)}, bf16[2,528,128]{2,1,0:T(8,128)(2,1)S(1)}, u32[]{:S(2)}, u32[]{:S(2)}) collective-permute-start(bf16[2,528,128]{2,1,0:T(8,128)(2,1)S(1)} %get-tuple-element.49), channel_id=1, source_target_pairs={{0,8},{8,16},{16,24},{24,0},{32,40},{40,48},{48,56},{56,32},{64,72... | collective-permute-start | bytes 811016 | tf_op jit(solution)/shard_map/ppermute | solution.py:243
  26.6 18.1 %collective-permute-start.7 = (bf16[2,528,128]{2,1,0:T(8,128)(2,1)S(1)}, bf16[2,528,128]{2,1,0:T(8,128)(2,1)S(1)}, u32[]{:S(2)}, u32[]{:S(2)}) collective-permute-start(bf16[2,528,128]{2,1,0:T(8,128)(2,1)S(1)} %get-tuple-element.50), channel_id=1, source_target_pairs={{0,16},{8,24},{16,0},{24,8},{32,48},{40,56},{48,32},{56,40},{64,80... | collective-permute-start | bytes 811016 | tf_op jit(solution)/shard_map/ppermute | solution.py:243
  29.4 15.7 %collective-permute-start.8 = (bf16[2,528,128]{2,1,0:T(8,128)(2,1)S(1)}, bf16[2,528,128]{2,1,0:T(8,128)(2,1)S(1)}, u32[]{:S(2)}, u32[]{:S(2)}) collective-permute-start(bf16[2,528,128]{2,1,0:T(8,128)(2,1)S(1)} %get-tuple-element.51), channel_id=1, source_target_pairs={{0,24},{8,0},{16,8},{24,16},{32,56},{40,32},{48,40},{56,48},{64,88... | collective-permute-start | bytes 811016 | tf_op jit(solution)/shard_map/ppermute | solution.py:243
  36.1 15.0 %collective-permute-start.5 = (bf16[2,528,128]{2,1,0:T(8,128)(2,1)S(1)}, bf16[2,528,128]{2,1,0:T(8,128)(2,1)S(1)}, u32[]{:S(2)}, u32[]{:S(2)}) collective-permute-start(bf16[2,528,128]{2,1,0:T(8,128)(2,1)S(1)} %get-tuple-element.48), channel_id=1, source_target_pairs={{0,16},{8,24},{16,0},{24,8},{32,48},{40,56},{48,32},{56,40},{64,80... | collective-permute-start | bytes 811016 | tf_op jit(solution)/shard_map/ppermute | solution.py:243
  38.6 14.7 %collective-permute-start.3 = (bf16[2,528,128]{2,1,0:T(8,128)(2,1)S(1)}, bf16[2,528,128]{2,1,0:T(8,128)(2,1)S(1)}, u32[]{:S(2)}, u32[]{:S(2)}) collective-permute-start(bf16[2,528,128]{2,1,0:T(8,128)(2,1)S(1)} %get-tuple-element.46), channel_id=1, source_target_pairs={{0,8},{8,16},{16,24},{24,0},{32,40},{40,48},{48,56},{56,32},{64,72... | collective-permute-start | bytes 811016 | tf_op jit(solution)/shard_map/ppermute | solution.py:243
  42.7 12.3 %collective-permute-start.4 = (bf16[2,528,128]{2,1,0:T(8,128)(2,1)S(1)}, bf16[2,528,128]{2,1,0:T(8,128)(2,1)S(1)}, u32[]{:S(2)}, u32[]{:S(2)}) collective-permute-start(bf16[2,528,128]{2,1,0:T(8,128)(2,1)S(1)} %get-tuple-element.47), channel_id=1, source_target_pairs={{0,24},{8,0},{16,8},{24,16},{32,56},{40,32},{48,40},{56,48},{64,88... | collective-permute-start | bytes 811016 | tf_op jit(solution)/shard_map/ppermute | solution.py:243

commit v4 on v3

--- a/solution.py
+++ b/solution.py
@@ -14,23 +14,15 @@
 YS = 4
 
 
-def pack_kernel(kv_ref, docs_ref, piece_ref, rows_ref, docs_vmem, sems):
+def pack_kernel(kv_ref, docs_ref, piece_ref, rows_ref):
     tok = kv_ref.shape[1]
-    copies = [
-        pltpu.make_async_copy(docs_ref, docs_vmem, sems.at[0]),
-        pltpu.make_async_copy(kv_ref.at[0], piece_ref.at[0:tok], sems.at[1]),
-        pltpu.make_async_copy(kv_ref.at[1], piece_ref.at[tok : 2 * tok], sems.at[2]),
-    ]
-    for copy in copies:
-        copy.start()
-    copies[0].wait()
-    docs = docs_vmem[...].astype(F32) + 1.0
+    piece_ref[0:tok] = kv_ref[0]
+    piece_ref[tok : 2 * tok] = kv_ref[1]
+    docs = docs_ref[...].astype(F32) + 1.0
     n = docs.shape[0]
     piece_ref[2 * tok :] = jnp.concatenate([docs, jnp.zeros((16 - n, HD), F32)], 0).astype(BF16)
     for t in range(n):
         rows_ref[t * HD : (t + 1) * HD] = jnp.broadcast_to(docs[t : t + 1], (HD, HD)).T
-    copies[1].wait()
-    copies[2].wait()
 
 
 def key_docs(piece_ref, lead, tok):
@@ -175,9 +167,9 @@
     tok = kv.shape[1]
     return pl.pallas_call(
         pack_kernel,
-        in_specs=[pl.BlockSpec(memory_space=pl.ANY)] * 2,
+        grid=(1,),
+        in_specs=[pl.BlockSpec(kv.shape, lambda i: (0, 0, 0)), pl.BlockSpec(docs.shape, lambda i: (0, 0))],
         out_specs=[VM, VM],
-        scratch_shapes=[pltpu.VMEM(docs.shape, docs.dtype), pltpu.SemaphoreType.DMA((3,))],
         out_shape=[jax.ShapeDtypeStruct((2 * tok + 16, HD), BF16), jax.ShapeDtypeStruct((tok, HD), F32)],
         compiler_params=params(),
         name="pack",
@@ -255,7 +247,7 @@
     carry = far(
         queries,
         rows,
-        [*near, both],
+        [near[1], near[0], near[2], both],
         [[(0, (0,)), (1, (0,)), (2, (0,))], [(0, (1,)), (1, (1,)), (2, (1,)), (3, (0,)), (3, (1,))]],
         carry,
         False,

time: 59.6 us -> 58.2 us (0.977)
  the two profiles are of different devices: /device:TPU:204 before, /device:TPU:92 now
where the time goes in v4:
time: 58.2 us; the launch traced here: 59.1 us
  starting transfers between devices  35.8 us (62%)
  Pallas kernels  15.1 us (26%)
  waiting for transfers between devices  5.14 us (9%)
  local copies, waits for them, and re-layouts  2.64 us (5%)
    ppermute x6, starting transfers between devices, across(): lax.ppermute(x, 'ctx', [(c, c - c % YS + (c + by) % YS) for c in range(si...  19 us
    ppermute x3, starting transfers between devices, up(): lax.ppermute(x, 'ctx', [(c, c + by * YS) for c in range(size - by * YS)])  16.9 us
    pallas_call x4, Pallas kernels, far(): pl.pallas_call(functools.partial(far_kernel, last, tiers, len(pieces)), i...  13.8 us
    ppermute x3, waiting for transfers between devices, up(): lax.ppermute(x, 'ctx', [(c, c + by * YS) for c in range(size - by * YS)])  2.71 us
    unnamed x8, local copies, waits for them, and re-layouts  2.63 us
    ppermute x6, waiting for transfers between devices, across(): lax.ppermute(x, 'ctx', [(c, c - c % YS + (c + by) % YS) for c in range(si...  2.43 us
  transfers between devices with their start and end apart: 9, of which 4 were waited for; matrix products, arithmetic and copies ran while one was open for 0% of the time, Pallas kernels for 19%

profile of v4, /device:TPU:92, one launch (start us, length us, event | category | flops | bytes accessed | tf_op | source)
XLA Modules:
  0.0 59.1 jit_solution(7642995109726740226)
XLA Ops:
  0.0 0.7 %copy-done.3 = s32[256]{0:T(256)S(1)} copy-done((s32[256]{0:T(256)S(1)}, s32[256]{0:T(256)}, u32[]{:S(2)}) %copy-start.3) | copy-done | bytes 1048
  0.7 0.9 %copy-done.2 = bf16[2,256,128]{2,1,0:T(8,128)(2,1)S(1)} copy-done((bf16[2,256,128]{2,1,0:T(8,128)(2,1)S(1)}, bf16[2,256,128]{2,1,0:T(8,128)(2,1)}, u32[]{:S(2)}) %copy-start.2) | copy-done | bytes 131096
  1.6 0.1 pack.1
  1.7 6.4 %collective-permute-start = (bf16[528,128]{1,0:T(8,128)(2,1)S(1)}, bf16[528,128]{1,0:T(8,128)(2,1)S(1)}, u32[]{:S(2)}, u32[]{:S(2)}) collective-permute-start(bf16[528,128]{1,0:T(8,128)(2,1)S(1)} %get-tuple-element.34.piece_ref.refs_0_), channel_id=1, source_target_pairs={{0,64},{8,72},{16,80},{24,88},{32,96},{40,104},{48,112},{56,120},{... | collective-permute-start | bytes 405512 | tf_op jit(solution)/shard_map/ppermute | solution.py:232
  8.1 3.8 %collective-permute-start.1 = (bf16[528,128]{1,0:T(8,128)(2,1)S(1)}, bf16[528,128]{1,0:T(8,128)(2,1)S(1)}, u32[]{:S(2)}, u32[]{:S(2)}) collective-permute-start(bf16[528,128]{1,0:T(8,128)(2,1)S(1)} %get-tuple-element.34.piece_ref.refs_0_), channel_id=1, source_target_pairs={{0,32},{8,40},{16,48},{24,56},{32,64},{40,72},{48,80},{56,88},{64,... | collective-permute-start | bytes 405512 | tf_op jit(solution)/shard_map/ppermute | solution.py:232
  11.9 0.0 copy-start
  11.9 1.0 %copy-done = bf16[256,1024]{1,0:T(8,128)(2,1)S(1)} copy-done((bf16[256,1024]{1,0:T(8,128)(2,1)S(1)}, bf16[256,1024]{1,0:T(8,128)(2,1)}, u32[]{:S(2)}) %copy-start) | copy-done | bytes 524312
  13.0 1.0 %own.1 = (f32[8,256,128]{2,1,0:T(8,128)S(1)}, f32[8,256,128]{2,1,0:T(8,128)S(1)}, f32[8,256,128]{2,1,0:T(8,128)S(1)}) custom-call(bf16[256,1024]{1,0:T(8,128)(2,1)S(1)} %copy-done, f32[256,128]{1,0:T(8,128)S(1)} %get-tuple-element.33.rows_ref.refs_1_, bf16[528,128]{1,0:T(8,128)(2,1)S(1)} %get-tuple-element.34.piece_ref.refs_0_), custom_call_target="tpu_custom_call" | custom-call | flops 268435456 | bytes 1048576 | tf_op jit(solution)/shard_map/own/pallas_call | solution.py:189
  14.0 0.0 copy-start.1
  14.0 0.7 %collective-permute-done.refs_3_.refs_0_.refs_2_ = bf16[528,128]{1,0:T(8,128)(2,1)S(1)} collective-permute-done((bf16[528,128]{1,0:T(8,128)(2,1)S(1)}, bf16[528,128]{1,0:T(8,128)(2,1)S(1)}, u32[]{:S(2)}, u32[]{:S(2)}) %collective-permute-start) | collective-permute-done | bytes 135200 | tf_op jit(solution)/shard_map/ppermute | solution.py:232
  14.7 1.9 %collective-permute-done.1.refs_2_.refs_1_ = bf16[528,128]{1,0:T(8,128)(2,1)S(1)} collective-permute-done((bf16[528,128]{1,0:T(8,128)(2,1)S(1)}, bf16[528,128]{1,0:T(8,128)(2,1)S(1)}, u32[]{:S(2)}, u32[]{:S(2)}) %collective-permute-start.1) | collective-permute-done | bytes 135200 | tf_op jit(solution)/shard_map/ppermute | solution.py:232
  16.6 6.6 %collective-permute-start.2 = (bf16[2,528,128]{2,1,0:T(8,128)(2,1)S(1)}, bf16[2,528,128]{2,1,0:T(8,128)(2,1)S(1)}, u32[]{:S(2)}, u32[]{:S(2)}) collective-permute-start(bf16[2,528,128]{2,1,0:T(8,128)(2,1)S(1)} %pad_maximum_fusion), channel_id=1, source_target_pairs={{0,64},{8,72},{16,80},{24,88},{32,96},{40,104},{48,112},{56,120},{... | collective-permute-start | bytes 811016 | tf_op jit(solution)/shard_map/ppermute | solution.py:232
  23.3 0.1 lay.3
  23.4 3.1 %collective-permute-start.6 = (bf16[2,528,128]{2,1,0:T(8,128)(2,1)S(1)}, bf16[2,528,128]{2,1,0:T(8,128)(2,1)S(1)}, u32[]{:S(2)}, u32[]{:S(2)}) collective-permute-start(bf16[2,528,128]{2,1,0:T(8,128)(2,1)S(1)} %get-tuple-element.49), channel_id=1, source_target_pairs={{0,16},{8,24},{16,0},{24,8},{32,48},{40,56},{48,32},{56,40},{64,80... | collective-permute-start | bytes 811016 | tf_op jit(solution)/shard_map/ppermute | solution.py:235
  26.5 4.1 %collective-permute-start.7 = (bf16[2,528,128]{2,1,0:T(8,128)(2,1)S(1)}, bf16[2,528,128]{2,1,0:T(8,128)(2,1)S(1)}, u32[]{:S(2)}, u32[]{:S(2)}) collective-permute-start(bf16[2,528,128]{2,1,0:T(8,128)(2,1)S(1)} %get-tuple-element.50), channel_id=1, source_target_pairs={{0,8},{8,16},{16,24},{24,0},{32,40},{40,48},{48,56},{56,32},{64,72... | collective-permute-start | bytes 811016 | tf_op jit(solution)/shard_map/ppermute | solution.py:235
  30.6 1.9 %collective-permute-start.8 = (bf16[2,528,128]{2,1,0:T(8,128)(2,1)S(1)}, bf16[2,528,128]{2,1,0:T(8,128)(2,1)S(1)}, u32[]{:S(2)}, u32[]{:S(2)}) collective-permute-start(bf16[2,528,128]{2,1,0:T(8,128)(2,1)S(1)} %get-tuple-element.51), channel_id=1, source_target_pairs={{0,24},{8,0},{16,8},{24,16},{32,56},{40,32},{48,40},{56,48},{64,88... | collective-permute-start | bytes 811016 | tf_op jit(solution)/shard_map/ppermute | solution.py:235
  32.6 0.0 copy-done.1
  32.6 2.1 %far.4 = (f32[8,256,128]{2,1,0:T(8,128)S(1)}, f32[8,256,128]{2,1,0:T(8,128)S(1)}, f32[8,256,128]{2,1,0:T(8,128)S(1)}) custom-call(bf16[256,1024]{1,0:T(8,128)(2,1)S(1)} %copy-done.1, f32[256,128]{1,0:T(8,128)S(1)} %get-tuple-element.33.rows_ref.refs_1_, bf16[528,128]{1,0:T(8,128)(2,1)S(1)} %collective-permute-done.1.refs_2_.refs_1_, ...), custom_call_target="tpu_custom_call" | custom-call | flops 536870912 | bytes 1048576 | tf_op jit(solution)/shard_map/far/pallas_call | solution.py:203
  34.7 0.1 collective-permute-done.2.refs_5_
  34.8 0.1 lay.2
  34.9 4.0 %collective-permute-start.5 = (bf16[2,528,128]{2,1,0:T(8,128)(2,1)S(1)}, bf16[2,528,128]{2,1,0:T(8,128)(2,1)S(1)}, u32[]{:S(2)}, u32[]{:S(2)}) collective-permute-start(bf16[2,528,128]{2,1,0:T(8,128)(2,1)S(1)} %get-tuple-element.48), channel_id=1, source_target_pairs={{0,16},{8,24},{16,0},{24,8},{32,48},{40,56},{48,32},{56,40},{64,80... | collective-permute-start | bytes 811016 | tf_op jit(solution)/shard_map/ppermute | solution.py:235
  38.9 3.3 %collective-permute-start.3 = (bf16[2,528,128]{2,1,0:T(8,128)(2,1)S(1)}, bf16[2,528,128]{2,1,0:T(8,128)(2,1)S(1)}, u32[]{:S(2)}, u32[]{:S(2)}) collective-permute-start(bf16[2,528,128]{2,1,0:T(8,128)(2,1)S(1)} %get-tuple-element.46), channel_id=1, source_target_pairs={{0,8},{8,16},{16,24},{24,0},{32,40},{40,48},{48,56},{56,32},{64,72... | collective-permute-start | bytes 811016 | tf_op jit(solution)/shard_map/ppermute | solution.py:235
  42.2 0.0 collective-permute-done.6.refs_2_
  42.2 2.6 %collective-permute-start.4 = (bf16[2,528,128]{2,1,0:T(8,128)(2,1)S(1)}, bf16[2,528,128]{2,1,0:T(8,128)(2,1)S(1)}, u32[]{:S(2)}, u32[]{:S(2)}) collective-permute-start(bf16[2,528,128]{2,1,0:T(8,128)(2,1)S(1)} %get-tuple-element.47), channel_id=1, source_target_pairs={{0,24},{8,0},{16,8},{24,16},{32,56},{40,32},{48,40},{56,48},{64,88... | collective-permute-start | bytes 811016 | tf_op jit(solution)/shard_map/ppermute | solution.py:235
  44.8 0.0 collective-permute-done.7.refs_3_
  44.8 2.4 %collective-permute-done.8.refs_4_ = bf16[2,528,128]{2,1,0:T(8,128)(2,1)S(1)} collective-permute-done((bf16[2,528,128]{2,1,0:T(8,128)(2,1)S(1)}, bf16[2,528,128]{2,1,0:T(8,128)(2,1)S(1)}, u32[]{:S(2)}, u32[]{:S(2)}) %collective-permute-start.8) | collective-permute-done | bytes 270368 | tf_op jit(solution)/shard_map/ppermute | solution.py:235
  47.2 5.5 %far.5 = (f32[8,256,128]{2,1,0:T(8,128)S(1)}, f32[8,256,128]{2,1,0:T(8,128)S(1)}, f32[8,256,128]{2,1,0:T(8,128)S(1)}) custom-call(bf16[256,1024]{1,0:T(8,128)(2,1)S(1)} %copy-done.1, f32[256,128]{1,0:T(8,128)S(1)} %get-tuple-element.33.rows_ref.refs_1_, bf16[2,528,128]{2,1,0:T(8,128)(2,1)S(1)} %collective-permute-done.6.refs_2_, ...), custom_call_target="tpu_custom_call" | custom-call | flops 2147483648 | bytes 1048576 | tf_op jit(solution)/shard_map/far/pallas_call | solution.py:203
  52.7 0.0 collective-permute-done.5.refs_2_
  52.7 2.2 %far.6 = (f32[8,256,128]{2,1,0:T(8,128)S(1)}, f32[8,256,128]{2,1,0:T(8,128)S(1)}, f32[8,256,128]{2,1,0:T(8,128)S(1)}) custom-call(bf16[256,1024]{1,0:T(8,128)(2,1)S(1)} %copy-done.1, f32[256,128]{1,0:T(8,128)S(1)} %get-tuple-element.33.rows_ref.refs_1_, bf16[2,528,128]{2,1,0:T(8,128)(2,1)S(1)} %collective-permute-done.5.refs_2_, ...), custom_call_target="tpu_custom_call" | custom-call | flops 536870912 | bytes 1048576 | tf_op jit(solution)/shard_map/far/pallas_call | solution.py:203
  54.9 0.0 collective-permute-done.3.refs_2_
  54.9 0.0 collective-permute-done.4.refs_3_
  54.9 4.0 %far.7 = bf16[256,1024]{1,0:T(8,128)(2,1)} custom-call(bf16[256,1024]{1,0:T(8,128)(2,1)S(1)} %copy-done.1, f32[256,128]{1,0:T(8,128)S(1)} %get-tuple-element.33.rows_ref.refs_1_, bf16[2,528,128]{2,1,0:T(8,128)(2,1)S(1)} %collective-permute-done.3.refs_2_, bf16[2,528,128]{2,1,0:T(8,128)(2,1)S(1)} %collective-permute-done.4.refs_3_, ...), custom_call_target="tpu_custom_call" | custom-call | flops 1073741824 | bytes 1048576 | tf_op jit(solution)/shard_map/far/pallas_call | solution.py:203
  (4 shorter events, 0.0 us)
Async XLA Ops:
  0.0 0.7 %copy-start.3 = (s32[256]{0:T(256)S(1)}, s32[256]{0:T(256)}, u32[]{:S(2)}) copy-start(s32[256]{0:T(256)} %param.5) | copy-start | bytes 3076
  0.7 0.9 %copy-start.2 = (bf16[2,256,128]{2,1,0:T(8,128)(2,1)S(1)}, bf16[2,256,128]{2,1,0:T(8,128)(2,1)}, u32[]{:S(2)}) copy-start(bf16[2,256,128]{2,1,0:T(8,128)(2,1)} %kv_ref.1) | copy-start | bytes 393220
  1.7 13.0 %collective-permute-start = (bf16[528,128]{1,0:T(8,128)(2,1)S(1)}, bf16[528,128]{1,0:T(8,128)(2,1)S(1)}, u32[]{:S(2)}, u32[]{:S(2)}) collective-permute-start(bf16[528,128]{1,0:T(8,128)(2,1)S(1)} %get-tuple-element.34.piece_ref.refs_0_), channel_id=1, source_target_pairs={{0,64},{8,72},{16,80},{24,88},{32,96},{40,104},{48,112},{56,120},{... | collective-permute-start | bytes 405512 | tf_op jit(solution)/shard_map/ppermute | solution.py:232
  8.1 8.5 %collective-permute-start.1 = (bf16[528,128]{1,0:T(8,128)(2,1)S(1)}, bf16[528,128]{1,0:T(8,128)(2,1)S(1)}, u32[]{:S(2)}, u32[]{:S(2)}) collective-permute-start(bf16[528,128]{1,0:T(8,128)(2,1)S(1)} %get-tuple-element.34.piece_ref.refs_0_), channel_id=1, source_target_pairs={{0,32},{8,40},{16,48},{24,56},{32,64},{40,72},{48,80},{56,88},{64,... | collective-permute-start | bytes 405512 | tf_op jit(solution)/shard_map/ppermute | solution.py:232
  11.9 1.0 %copy-start = (bf16[256,1024]{1,0:T(8,128)(2,1)S(1)}, bf16[256,1024]{1,0:T(8,128)(2,1)}, u32[]{:S(2)}) copy-start(bf16[256,1024]{1,0:T(8,128)(2,1)} %refs_0_.7) | copy-start | bytes 1572868
  14.0 18.6 %copy-start.1 = (bf16[256,1024]{1,0:T(8,128)(2,1)S(1)}, bf16[256,1024]{1,0:T(8,128)(2,1)}, u32[]{:S(2)}) copy-start(bf16[256,1024]{1,0:T(8,128)(2,1)} %refs_0_.7) | copy-start | bytes 1572868
  16.6 18.2 %collective-permute-start.2 = (bf16[2,528,128]{2,1,0:T(8,128)(2,1)S(1)}, bf16[2,528,128]{2,1,0:T(8,128)(2,1)S(1)}, u32[]{:S(2)}, u32[]{:S(2)}) collective-permute-start(bf16[2,528,128]{2,1,0:T(8,128)(2,1)S(1)} %pad_maximum_fusion), channel_id=1, source_target_pairs={{0,64},{8,72},{16,80},{24,88},{32,96},{40,104},{48,112},{56,120},{... | collective-permute-start | bytes 811016 | tf_op jit(solution)/shard_map/ppermute | solution.py:232
  23.4 18.8 %collective-permute-start.6 = (bf16[2,528,128]{2,1,0:T(8,128)(2,1)S(1)}, bf16[2,528,128]{2,1,0:T(8,128)(2,1)S(1)}, u32[]{:S(2)}, u32[]{:S(2)}) collective-permute-start(bf16[2,528,128]{2,1,0:T(8,128)(2,1)S(1)} %get-tuple-element.49), channel_id=1, source_target_pairs={{0,16},{8,24},{16,0},{24,8},{32,48},{40,56},{48,32},{56,40},{64,80... | collective-permute-start | bytes 811016 | tf_op jit(solution)/shard_map/ppermute | solution.py:235
  26.5 18.3 %collective-permute-start.7 = (bf16[2,528,128]{2,1,0:T(8,128)(2,1)S(1)}, bf16[2,528,128]{2,1,0:T(8,128)(2,1)S(1)}, u32[]{:S(2)}, u32[]{:S(2)}) collective-permute-start(bf16[2,528,128]{2,1,0:T(8,128)(2,1)S(1)} %get-tuple-element.50), channel_id=1, source_target_pairs={{0,8},{8,16},{16,24},{24,0},{32,40},{40,48},{48,56},{56,32},{64,72... | collective-permute-start | bytes 811016 | tf_op jit(solution)/shard_map/ppermute | solution.py:235
  30.6 16.6 %collective-permute-start.8 = (bf16[2,528,128]{2,1,0:T(8,128)(2,1)S(1)}, bf16[2,528,128]{2,1,0:T(8,128)(2,1)S(1)}, u32[]{:S(2)}, u32[]{:S(2)}) collective-permute-start(bf16[2,528,128]{2,1,0:T(8,128)(2,1)S(1)} %get-tuple-element.51), channel_id=1, source_target_pairs={{0,24},{8,0},{16,8},{24,16},{32,56},{40,32},{48,40},{56,48},{64,88... | collective-permute-start | bytes 811016 | tf_op jit(solution)/shard_map/ppermute | solution.py:235
  34.9 17.8 %collective-permute-start.5 = (bf16[2,528,128]{2,1,0:T(8,128)(2,1)S(1)}, bf16[2,528,128]{2,1,0:T(8,128)(2,1)S(1)}, u32[]{:S(2)}, u32[]{:S(2)}) collective-permute-start(bf16[2,528,128]{2,1,0:T(8,128)(2,1)S(1)} %get-tuple-element.48), channel_id=1, source_target_pairs={{0,16},{8,24},{16,0},{24,8},{32,48},{40,56},{48,32},{56,40},{64,80... | collective-permute-start | bytes 811016 | tf_op jit(solution)/shard_map/ppermute | solution.py:235
  38.9 16.0 %collective-permute-start.3 = (bf16[2,528,128]{2,1,0:T(8,128)(2,1)S(1)}, bf16[2,528,128]{2,1,0:T(8,128)(2,1)S(1)}, u32[]{:S(2)}, u32[]{:S(2)}) collective-permute-start(bf16[2,528,128]{2,1,0:T(8,128)(2,1)S(1)} %get-tuple-element.46), channel_id=1, source_target_pairs={{0,8},{8,16},{16,24},{24,0},{32,40},{40,48},{48,56},{56,32},{64,72... | collective-permute-start | bytes 811016 | tf_op jit(solution)/shard_map/ppermute | solution.py:235
  42.2 12.7 %collective-permute-start.4 = (bf16[2,528,128]{2,1,0:T(8,128)(2,1)S(1)}, bf16[2,528,128]{2,1,0:T(8,128)(2,1)S(1)}, u32[]{:S(2)}, u32[]{:S(2)}) collective-permute-start(bf16[2,528,128]{2,1,0:T(8,128)(2,1)S(1)} %get-tuple-element.47), channel_id=1, source_target_pairs={{0,24},{8,0},{16,8},{24,16},{32,56},{40,32},{48,40},{56,48},{64,88... | collective-permute-start | bytes 811016 | tf_op jit(solution)/shard_map/ppermute | solution.py:235
